TPU v7x, 128 devices: a whole 4x4x4 slice. The times are simulated.
128 devices in a mesh: fsdp: 8 (over y_lo, z), replica: 16 (over y_hi, x, core).
Axes of the slice: x: 4, y: 4 (y_hi: 2, y_lo: 2; y = y_hi * 2 + y_lo), z: 4, core: 2. Of those that a mesh axis runs over, the one named last changes fastest.
Arguments:
- out_weight: bfloat16 [2, 512, 16384], P(None, None, 'fsdp'), may hold values from -6 to 6
- down_weight: bfloat16 [2, 1024, 16384], P(None, None, 'fsdp'), may hold values from -6 to 6
- layer_share: int32 [16], replicated, may hold values from 0 to 15, each once
- rank_map: int32 [8], replicated, may hold values from 0 to 7, each once
Outputs:
- out_quant: bfloat16 [8, 128, 16384], P('fsdp')
- out_scales: bfloat16 [8, 128, 128], P('fsdp')
- down_quant: bfloat16 [8, 256, 16384], P('fsdp')
- down_scales: bfloat16 [8, 256, 128], P('fsdp')
Inputs may be any that keep to these rules, and one draw needn't show every extreme that they name: `layer_share`: each block number appears once. `rank_map`: each rank appears once.
All inputs are finite; a program needn't handle non-finite values.
Results may differ from a plain program's by a relative error of at most 0.012.
Values may be sent and summed in bfloat16 or wider, within the bound.
No kernel may reach another device: no remote copies, remote signals or barrier semaphores. Data moves between devices by JAX's collectives and lax.ppermute only.
A program may use at most 128 MiB of HBM per device.

v0:
```python
import math

import jax
import jax.numpy as jnp
from jax import lax
from jax.sharding import PartitionSpec as P


def sylvester(order):
    index = jnp.arange(order, dtype=jnp.int32)
    signs = jnp.ones((order, order), jnp.float32)
    level = 1
    while level < order:
        bit_row = index // level % 2
        signs = signs * (1 - 2 * (bit_row[:, None] * bit_row[None, :])).astype(jnp.float32)
        level = level * 2
    return signs / math.sqrt(order)


def rotate_cast(weights_in):
    columns = weights_in.shape[-1]
    side_len = math.isqrt(columns)
    rotation = sylvester(side_len)
    squares = weights_in.reshape(-1, side_len, side_len).astype(jnp.float32)
    half_turn = jnp.einsum("ab,nbc->nac", rotation, squares, precision=lax.Precision.HIGHEST)
    rotated = jnp.einsum("nac,cd->nad", half_turn, rotation, precision=lax.Precision.HIGHEST)
    largest = jnp.max(jnp.abs(rotated), axis=2, keepdims=True)
    block_scale = (largest + 1e-06).astype(jnp.bfloat16)
    quantized = (rotated / block_scale.astype(jnp.float32)).astype(jnp.bfloat16)
    return (
        quantized.reshape(weights_in.shape),
        block_scale.reshape(weights_in.shape[:-1] + (side_len,)),
    )


def share_rows(weights, layer_share, rank_map):
    groups = lax.axis_size("fsdp")
    copies = lax.axis_size("replica")
    layers_all, rows_all, cols_local = weights.shape
    rank_rows = rows_all // groups
    page_rows = layers_all * rank_rows // copies
    first_row = layer_share[lax.axis_index("replica")] * page_rows
    layer_at = first_row // rank_rows
    offset_row = first_row % rank_rows
    chosen = lax.dynamic_index_in_dim(weights, layer_at, 0, keepdims=False)
    chosen = chosen.reshape(groups, rank_rows, cols_local)
    chosen = lax.dynamic_slice_in_dim(chosen, offset_row, page_rows, 1)
    return jnp.take(chosen, rank_map, axis=0)


def shards(out_weight, down_weight, layer_share, rank_map):
    send_out = share_rows(out_weight, layer_share, rank_map)
    quant_out, scale_out = rotate_cast(
        lax.all_to_all(send_out, "fsdp", split_axis=0, concat_axis=2, tiled=True)
    )
    send_down = share_rows(down_weight, layer_share, rank_map)
    quant_down, scale_down = rotate_cast(
        lax.all_to_all(send_down, "fsdp", split_axis=0, concat_axis=2, tiled=True)
    )
    quant_out, scale_out = (
        lax.all_gather(quant_out, "replica", axis=1, tiled=True),
        lax.all_gather(scale_out, "replica", axis=1, tiled=True),
    )
    quant_down, scale_down = (
        lax.all_gather(quant_down, "replica", axis=1, tiled=True),
        lax.all_gather(scale_down, "replica", axis=1, tiled=True),
    )
    return (quant_out, scale_out, quant_down, scale_down)


def solution(mesh):
    return jax.shard_map(
        shards,
        mesh=mesh,
        in_specs=(P(None, None, "fsdp"), P(None, None, "fsdp"), P(), P()),
        out_specs=(
            P("fsdp", None, None),
            P("fsdp", None, None),
            P("fsdp", None, None),
            P("fsdp", None, None),
        ),
        check_vma=False,
    )
```

profile of v0, /device:TPU:1, one launch (start us, length us, event | category | flops | bytes accessed | tf_op | source)
XLA Modules:
  0.0 182.2 jit_solution(3792777682376161915)
XLA Ops:
  7.2 0.7 compare_select_fusion
  7.8 0.7 compare_and_fusion
  8.5 1.2 dynamic_slice.18
  10.4 1.7 constant_dynamic-slice_fusion.3
  12.3 0.6 gather_fusion
  12.9 0.8 broadcast_select_fusion.1
  13.7 6.9 %all-to-all-start = ((bf16[8,8,2048]{2,1,0:T(8,128)(2,1)}), bf16[8,8,2048]{2,1,0:T(8,128)(2,1)S(1)}, u32[]{:S(2)}, u32[]{:S(2)}) async-start(bf16[8,8,2048]{2,1,0:T(8,128)(2,1)} %broadcast_select_fusion.1), calls=%async_computation | async-start | bytes 524288 | tf_op jit(solution)/shard_map/all_to_all | solution.py:54
  20.6 6.0 %all-to-all-done = bf16[8,8,2048]{2,1,0:T(8,128)(2,1)S(1)} async-done(((bf16[8,8,2048]{2,1,0:T(8,128)(2,1)}), bf16[8,8,2048]{2,1,0:T(8,128)(2,1)S(1)}, u32[]{:S(2)}, u32[]{:S(2)}) %all-to-all-start) | async-done | bytes 262176 | tf_op jit(solution)/shard_map/all_to_all | solution.py:54
  26.6 0.1 copy.10
  26.8 0.1 reshape.374
  26.9 0.6 convolution_bitcast_fusion.1
  27.6 0.7 abs_reduce_fusion.1
  28.4 0.2 copy.14
  28.6 0.8 reshape.375
  30.1 2.5 %constant_dynamic-slice_fusion.1 = bf16[1,1024,2048]{2,1,0:T(8,128)(2,1)S(1)} fusion(bf16[2,1024,2048]{2,1,0:T(8,128)(2,1)} %param.5, s32[]{:T(128)S(6)} %select_n.328), kind=kLoop, calls=%fused_computation.48 | loop fusion | bytes 8388612 | tf_op jit(solution)/shard_map/jit(dynamic_index_in_dim)/dynamic_slice | solution.py:45
  32.6 0.1 constant_dynamic-slice_fusion
  32.8 0.6 gather_fusion.1
  33.5 9.9 %all_to_all.30 = bf16[8,16,2048]{2,1,0:T(8,128)(2,1)S(1)} all-to-all(bf16[8,16,2048]{2,1,0:T(8,128)(2,1)S(1)} %broadcast_select_fusion), channel_id=1, replica_groups=mesh['fsdp'=8,'replica'=16] {'fsdp'}, dimensions={0} | all-to-all | bytes 1048576 | tf_op jit(solution)/shard_map/all_to_all | solution.py:58
  43.4 0.3 copy.15
  43.7 0.2 reshape.377
  44.0 0.9 convolution_bitcast_fusion
  44.9 1.2 abs_reduce_fusion
  46.1 0.1 divide_convert_fusion
  46.2 0.3 copy.19
  46.5 1.0 reshape.378
  47.5 29.5 %all-gather = bf16[128,128]{1,0:T(8,128)(2,1)S(1)} all-gather(bf16[8,128]{1,0:T(8,128)(2,1)S(1)} %get-tuple-element.7), channel_id=2, replica_groups=mesh['fsdp'=8,'replica'=16] {'replica'}, dimensions={0}, use_global_device_ids=true | all-gather | bytes 34816 | tf_op jit(solution)/shard_map/all_gather | solution.py:62
  77.1 19.4 %all-gather.1 = bf16[256,128]{1,0:T(8,128)(2,1)S(1)} all-gather(bf16[16,128]{1,0:T(8,128)(2,1)S(1)} %get-tuple-element.5), channel_id=3, replica_groups=mesh['fsdp'=8,'replica'=16] {'replica'}, dimensions={0}, use_global_device_ids=true | all-gather | bytes 69632 | tf_op jit(solution)/shard_map/all_gather | solution.py:66
  96.5 65.4 %all-gather.7.cloned.1.call-done = bf16[1,256,16384]{2,1,0:T(8,128)(2,1)} async-done(((bf16[1,16,16384]{2,1,0:T(8,128)(2,1)}), bf16[1,256,16384]{2,1,0:T(8,128)(2,1)}) %all-gather.7.cloned.1.call-update) | async-done | bytes 8388624 | tf_op jit(solution)/shard_map/all_gather | solution.py:65
  161.9 4.6 %copy.32 = bf16[1,128,16384]{2,1,0:T(8,128)(2,1)} copy(bf16[1,128,16384]{2,1,0:T(8,128)(2,1)} %all-gather.5.cloned.1.call-done) | data formatting | bytes 8388608
  166.4 0.6 copy.33
  167.0 7.7 %copy.34 = bf16[1,256,16384]{2,1,0:T(8,128)(2,1)} copy(bf16[1,256,16384]{2,1,0:T(8,128)(2,1)} %all-gather.7.cloned.1.call-done) | data formatting | bytes 16777216
  174.7 0.6 copy.35
  (15 shorter events, 0.4 us)
Async XLA Ops:
  13.7 13.0 %all-to-all-start = ((bf16[8,8,2048]{2,1,0:T(8,128)(2,1)}), bf16[8,8,2048]{2,1,0:T(8,128)(2,1)S(1)}, u32[]{:S(2)}, u32[]{:S(2)}) async-start(bf16[8,8,2048]{2,1,0:T(8,128)(2,1)} %broadcast_select_fusion.1), calls=%async_computation | async-start | bytes 524288 | tf_op jit(solution)/shard_map/all_to_all | solution.py:54
  20.5 76.0 %all-gather.5.cloned.1.call-start = ((), (), s32[]{:S(2)}) async-start(), calls=%async_computation.2 | async-start | bytes 4456448 | tf_op jit(solution)/shard_map/all_gather | solution.py:61
  29.4 132.5 %all-gather.7.cloned.1.call-start = ((), (), s32[]{:S(2)}) async-start(), calls=%async_computation.3 | async-start | bytes 8912896 | tf_op jit(solution)/shard_map/all_gather | solution.py:65
Sparse Core Ops, SparseCore 0:
  29.5 57.6 all-gather.4
  90.2 71.5 all-gather.6
where the time goes:
time: 183 us; the launch traced here: 182 us
  waiting for transfers between devices  71.4 us (39%)
  blocking collectives  58.9 us (32%)
  local copies, waits for them, and re-layouts  23.4 us (13%)
  between operations  15.6 us (9%)
  starting transfers between devices  6.95 us (4%)
  matrix products  3.42 us (2%)
  other arithmetic  2.44 us (1%)
    all_gather x1, waiting for transfers between devices, shards(): lax.all_gather(quant_down, 'replica', axis=1, tiled=True)  65.4 us
    all_gather x1, blocking collectives, shards(): lax.all_gather(scale_out, 'replica', axis=1, tiled=True)  29.5 us
    all_gather x1, blocking collectives, shards(): lax.all_gather(scale_down, 'replica', axis=1, tiled=True)  19.4 us
    unnamed x4, local copies, waits for them, and re-layouts  13.5 us
    all_to_all x1, blocking collectives, shards(): lax.all_to_all(send_down, 'fsdp', split_axis=0, concat_axis=2, tiled=True)  9.93 us
    all_to_all x1, starting transfers between devices, shards(): lax.all_to_all(send_out, 'fsdp', split_axis=0, concat_axis=2, tiled=True)  6.88 us
    all_to_all x1, waiting for transfers between devices, shards(): lax.all_to_all(send_out, 'fsdp', split_axis=0, concat_axis=2, tiled=True)  6.02 us
    dynamic_slice x2, local copies, waits for them, and re-layouts, share_rows(): chosen = lax.dynamic_index_in_dim(weights, layer_at, 0, keepdims=False)  4.23 us
  transfers between devices with their start and end apart: 3, of which 2 were waited for; matrix products, arithmetic and copies ran while one was open for 4% of the time, Pallas kernels for 0%

commit v1 on v0

v1 whole, which is shorter than its diff:
```python
import functools
import math

import jax
import jax.numpy as jnp
import numpy as np
from jax import lax
from jax.experimental import pallas as pl
from jax.experimental.pallas import tpu as pltpu
from jax.sharding import PartitionSpec as P

SIDE = 128
UNIT = 16
LOCAL = 2048
BLOCKS = LOCAL // SIDE
SHARDS = 8
PARTS = ((0, 1, 0, 2), (1, 1, 2, 2))
VMEM = 40 * 2**20


def signs(order):
    h = np.ones((1, 1), np.float32)
    while h.shape[0] < order:
        h = np.block([[h, h], [h, -h]])
    return h


def two_blocks():
    h = signs(SIDE)
    z = np.zeros_like(h)
    return jnp.asarray(np.block([[h, z], [z, h]]), jnp.bfloat16)


def butterflies(values):
    span = 1
    values = list(values)
    while span < len(values):
        for i in range(len(values)):
            if i & span == 0:
                lo, hi = values[i], values[i + span]
                values[i], values[i + span] = lo + hi, lo - hi
        span *= 2
    return values


def pick_kernel(part, share, ranks, q_ref, out_hbm, down_hbm, send, pairs, sems):
    o0, no, d0, nd = part
    q = q_ref[0]
    copies = []
    for u in range(no):
        for h in range(2):
            block = share[4 * q + 2 * (o0 + u) + h]
            for f in range(SHARDS):
                row = ranks[f] * 64 + lax.rem(block, 8) // 2 * 16
                c = pltpu.make_async_copy(
                    out_hbm.at[block // 8, pl.ds(pl.multiple_of(row, 16), 16), :],
                    pairs.at[u, h, f],
                    sems.at[len(copies)],
                )
                c.start()
                copies.append(c)
    for u in range(nd):
        block = share[4 * q + d0 + u]
        for f in range(SHARDS):
            row = ranks[f] * 128 + lax.rem(block, 8) * 16
            c = pltpu.make_async_copy(
                down_hbm.at[block // 8, pl.ds(pl.multiple_of(row, 16), 16), :],
                send.at[f, pl.ds((no + u) * UNIT, UNIT), :],
                sems.at[len(copies)],
            )
            c.start()
            copies.append(c)
    for c in copies:
        c.wait()
    for u in range(no):
        odd = [lax.rem(share[4 * q + 2 * (o0 + u) + h], 2) == 1 for h in range(2)]
        for f in range(SHARDS):
            halves = []
            for h in range(2):
                rows = pairs[u, h, f].astype(jnp.float32)
                halves.append(jnp.where(odd[h], rows[8:], rows[:8]))
            send[f, pl.ds(u * UNIT, UNIT), :] = jnp.concatenate(halves, 0).astype(
                jnp.bfloat16
            )


def pick(part, share, ranks, q, out_weight, down_weight):
    o0, no, d0, nd = part
    n = (no * 2 + nd) * SHARDS
    shape = (SHARDS, (no + nd) * UNIT, LOCAL)
    return pl.pallas_call(
        functools.partial(pick_kernel, part),
        grid_spec=pltpu.PrefetchScalarGridSpec(
            num_scalar_prefetch=3,
            grid=(),
            in_specs=[pl.BlockSpec(memory_space=pl.ANY)] * 2,
            out_specs=pl.BlockSpec(memory_space=pltpu.VMEM),
            scratch_shapes=[
                pltpu.VMEM((max(no, 1), 2, SHARDS, UNIT, LOCAL), jnp.bfloat16),
                pltpu.SemaphoreType.DMA((n,)),
            ],
        ),
        out_shape=jax.ShapeDtypeStruct(shape, jnp.bfloat16),
        compiler_params=pltpu.CompilerParams(vmem_limit_bytes=VMEM),
        cost_estimate=pl.CostEstimate(
            flops=0, bytes_accessed=3 * math.prod(shape) * 2, transcendentals=0
        ),
        name="pick_rows",
    )(share, ranks, q, out_weight, down_weight)


def rotate_unit(refs, rot, quant, scales, work):
    first = 0
    for ref in refs:

        def shard(s, _, ref=ref, first=first):
            x = ref[s]
            stack = jnp.concatenate(
                [x[:, c * 256 : (c + 1) * 256] for c in range(BLOCKS // 2)], 0
            )
            y = jnp.dot(stack, rot, preferred_element_type=jnp.float32)
            parts = [
                y[c * UNIT : (c + 1) * UNIT, h * SIDE : (h + 1) * SIDE]
                for c in range(BLOCKS // 2)
                for h in range(2)
            ]
            parts = butterflies(parts)
            for k in range(BLOCKS):
                work[(first + s) * BLOCKS + k] = parts[k]
            return 0

        lax.fori_loop(0, ref.shape[0], shard, 0)
        first += ref.shape[0]

    lane = lax.broadcasted_iota(jnp.int32, (UNIT, SIDE), 1)

    def column(k, top):
        parts = butterflies([work[f * BLOCKS + k] for f in range(SHARDS)])
        for f in range(SHARDS):
            a = f * BLOCKS + k
            y = parts[f]
            m = jnp.max(jnp.abs(y), axis=1, keepdims=True) * (1.0 / SIDE)
            s = (m + 1e-06).astype(jnp.bfloat16).astype(jnp.float32)
            r = 1.0 / (s * SIDE)
            quant[:, pl.ds(pl.multiple_of(a * SIDE, SIDE), SIDE)] = (y * r).astype(
                jnp.bfloat16
            )
            top = jnp.where(lane == a, m, top)
        return top

    top = lax.fori_loop(0, BLOCKS, column, jnp.zeros((UNIT, SIDE), jnp.float32))
    scales[...] = (top + 1e-06).astype(jnp.bfloat16)


def rotate_kernel(counts, no, nd, n_alias, q_ref, *refs):
    groups, at = [], 0
    for n in counts:
        groups.append(refs[at : at + n])
        at += n
    rot_ref = refs[at]
    at += 1 + n_alias
    outs = refs[at : at + 4]
    work = refs[at + 4]
    u, g = pl.program_id(0), pl.program_id(1)
    for i, group in enumerate(groups):

        @pl.when((g == i) & (u < no))
        def _(group=group):
            rotate_unit(group, rot_ref[...], outs[0], outs[1], work)

        @pl.when((g == i) & (u >= no))
        def _(group=group):
            rotate_unit(group, rot_ref[...], outs[2], outs[3], work)


def rotate(part, groups, qs, rot, before):
    o0, no, d0, nd = part
    n_groups = len(groups)
    flat = [b for group in groups for b in group]

    def out_at(u, g, q):
        last = u >= no
        return (
            jnp.where(last, 2 * q[n_groups - 1] + o0 + no - 1, 2 * q[g] + o0 + u),
            0,
        )

    def down_at(u, g, q):
        early = u < no
        return jnp.where(early, 4 * q[0] + d0, 4 * q[g] + d0 + u - no), 0

    in_specs = [
        pl.BlockSpec((b.shape[0], UNIT, LOCAL), lambda u, g, q: (0, u, 0)) for b in flat
    ]
    in_specs.append(pl.BlockSpec((256, 256), lambda u, g, q: (0, 0)))
    operands = flat + [rot]
    aliases = {}
    if before is not None:
        for i, b in enumerate(before):
            aliases[1 + len(operands)] = i
            operands.append(b)
            in_specs.append(pl.BlockSpec(memory_space=pl.ANY))
    columns = SHARDS * LOCAL
    shapes = [(128, columns), (128, SIDE), (256, columns), (256, SIDE)]
    maps = [out_at, out_at, down_at, down_at]
    elements = n_groups * (no + nd) * UNIT * columns
    return pl.pallas_call(
        functools.partial(
            rotate_kernel, [len(g) for g in groups], no, nd, len(aliases)
        ),
        grid_spec=pltpu.PrefetchScalarGridSpec(
            num_scalar_prefetch=1,
            grid=(no + nd, n_groups),
            in_specs=in_specs,
            out_specs=[
                pl.BlockSpec((UNIT, s[1]), m) for s, m in zip(shapes, maps)
            ],
            scratch_shapes=[
                pltpu.VMEM((SHARDS * BLOCKS, UNIT, SIDE), jnp.float32)
            ],
        ),
        out_shape=[jax.ShapeDtypeStruct(s, jnp.bfloat16) for s in shapes],
        input_output_aliases=aliases,
        compiler_params=pltpu.CompilerParams(vmem_limit_bytes=VMEM),
        cost_estimate=pl.CostEstimate(
            flops=elements * 256, bytes_accessed=elements * 4, transcendentals=0
        ),
        name="rotate_cast",
    )(qs, *operands)


def replica_steps(step):
    pairs = []
    for y in range(2):
        for x in range(4):
            for c in range(2):
                y2, x2, c2 = step(y, x, c)
                pairs.append(((y * 4 + x) * 2 + c, (y2 * 4 + x2 % 4) * 2 + c2))
    return pairs


RIGHT = replica_steps(lambda y, x, c: (y, x + 1, c))
LEFT = replica_steps(lambda y, x, c: (y, x + 3, c))
OTHER = replica_steps(lambda y, x, c: (y, x, 1 - c))


def shards(out_weight, down_weight, layer_share, rank_map):
    here = lax.axis_index("replica")
    q = here % 4
    qs = lambda *flips: jnp.stack([q ^ f for f in flips]).astype(jnp.int32)
    rot = two_blocks()
    sends = [
        pick(part, layer_share, rank_map, qs(0), out_weight, down_weight)
        for part in PARTS
    ]
    done = None
    half = SHARDS // 2
    late = []
    for part, send in zip(PARTS, sends):
        own = lax.all_to_all(send, "fsdp", split_axis=0, concat_axis=0, tiled=True)
        from_left = lax.ppermute(own[:half], "replica", RIGHT)
        from_right = lax.ppermute(own[half:], "replica", LEFT)
        other = lax.ppermute(own, "replica", OTHER)
        other_left = lax.ppermute(from_left, "replica", OTHER)
        other_right = lax.ppermute(from_right, "replica", OTHER)
        late.append((part, own, other, from_left, from_right, other_left, other_right))
    for part, own, other, l, r, ol, orr in late:
        done = rotate(part, [[own], [other]], qs(0, 1), rot, done)
        done = rotate(part, [[l, r], [ol, orr]], qs(2, 3), rot, done)
    return tuple(d[None] for d in done)


def solution(mesh):
    return jax.shard_map(
        shards,
        mesh=mesh,
        in_specs=(P(None, None, "fsdp"), P(None, None, "fsdp"), P(), P()),
        out_specs=(P("fsdp", None, None),) * 4,
        check_vma=False,
    )
```

time: 183 us -> 181 us (0.989)
  Pallas kernels: 0 us -> 102 us
  blocking collectives: 58.9 us -> 0 us
  waiting for transfers between devices: 71.4 us -> 41.5 us
  between operations: 15.6 us -> 0.73 us
  starting transfers between devices: 6.95 us -> 20.7 us
  local copies, waits for them, and re-layouts: 23.4 us -> 14.9 us
  matrix products: 3.42 us -> 0 us
  other arithmetic: 2.44 us -> 0.15 us
    pallas_call x0 -> x6, Pallas kernels: none -> 102 us  [the longest x4 93.2 us: rotate(): pl.pallas_call(functools.partial(rotate_kernel, [len(g) for g in groups],...]
    all_gather x2 -> x0, waiting for transfers between devices: 65.4 us -> none  [the longest x1 65.4 us: shards(): lax.all_gather(quant_down, 'replica', axis=1, tiled=True)]
    all_gather x2 -> x0, blocking collectives: 49 us -> none  [the longest x1 29.5 us: shards(): lax.all_gather(scale_out, 'replica', axis=1, tiled=True)]
    all_to_all x1 -> x2, waiting for transfers between devices: 6.02 us -> 25.5 us  [shards(): own = lax.all_to_all(send, 'fsdp', split_axis=0, concat_axis=0, tiled=True)]
    ppermute x0 -> x10, waiting for transfers between devices: none -> 15.9 us  [the longest x2 15.7 us: shards(): from_left = lax.ppermute(own[:half], 'replica', RIGHT)]
    ppermute x0 -> x10, starting transfers between devices: none -> 10.1 us  [the longest x2 2.93 us: shards(): from_right = lax.ppermute(own[half:], 'replica', LEFT)]
    all_to_all x1 -> x0, blocking collectives: 9.93 us -> none  [shards(): lax.all_to_all(send_down, 'fsdp', split_axis=0, concat_axis=2, tiled=True)]
    dynamic_slice x5 -> x0, local copies, waits for them, and re-layouts: 5.71 us -> none  [the longest x2 4.23 us: share_rows(): chosen = lax.dynamic_index_in_dim(weights, layer_at, 0, keepdims=False)]
  transfers between devices with their start and end apart: 3 -> 12, of which waited for: 2 -> 4; matrix products, arithmetic and copies ran while one was open for 4% -> 1% of each run, Pallas kernels for 0% -> 41%
where the time goes in v1:
time: 181 us; the launch traced here: 180 us
  Pallas kernels  102 us (56%)
  waiting for transfers between devices  41.5 us (23%)
  starting transfers between devices  20.7 us (11%)
  local copies, waits for them, and re-layouts  14.9 us (8%)
    pallas_call x4, Pallas kernels, rotate(): pl.pallas_call(functools.partial(rotate_kernel, [len(g) for g in groups],...  93.2 us
    all_to_all x2, waiting for transfers between devices, shards(): own = lax.all_to_all(send, 'fsdp', split_axis=0, concat_axis=0, tiled=True)  25.5 us
    ppermute x2, waiting for transfers between devices, shards(): from_left = lax.ppermute(own[:half], 'replica', RIGHT)  15.7 us
    unnamed x20, local copies, waits for them, and re-layouts  13.6 us
    all_to_all x2, starting transfers between devices, shards(): own = lax.all_to_all(send, 'fsdp', split_axis=0, concat_axis=0, tiled=True)  10.6 us
    pallas_call x2, Pallas kernels, pick(): pl.pallas_call(functools.partial(pick_kernel, part), grid_spec=pltpu.Pref...  8.99 us
  transfers between devices with their start and end apart: 12, of which 4 were waited for; matrix products, arithmetic and copies ran while one was open for 1% of the time, Pallas kernels for 41%

profile of v1, /device:TPU:1, one launch (start us, length us, event | category | flops | bytes accessed | tf_op | source)
XLA Modules:
  0.0 180.2 jit_solution(17372772534352345858)
XLA Ops:
  0.7 3.4 %copy-done = bf16[2,1024,2048]{2,1,0:T(8,128)(2,1)S(1)} copy-done((bf16[2,1024,2048]{2,1,0:T(8,128)(2,1)S(1)}, bf16[2,1024,2048]{2,1,0:T(8,128)(2,1)}, u32[]{:S(2)}) %copy-start) | copy-done | bytes 8388632
  4.0 2.2 %copy-done.2 = bf16[2,512,2048]{2,1,0:T(8,128)(2,1)S(1)} copy-done((bf16[2,512,2048]{2,1,0:T(8,128)(2,1)S(1)}, bf16[2,512,2048]{2,1,0:T(8,128)(2,1)}, u32[]{:S(2)}) %copy-start.2) | copy-done | bytes 4194328
  6.2 0.7 copy-done.6
  6.9 0.7 copy-done.8
  7.5 5.1 %pick_rows.3 = bf16[8,48,2048]{2,1,0:T(8,128)(2,1)} custom-call(s32[16]{0:T(128)S(1)} %copy-done.6, s32[8]{0:T(128)S(1)} %copy-done.8, s32[1]{0:T(128)} %bitcast.2.q_ref, bf16[2,512,2048]{2,1,0:T(8,128)(2,1)S(1)} %copy-done.2, bf16[2,1024,2048]{2,1,0:T(8,128)(2,1)S(1)} %copy-done), custom_call_target="tpu_custom_call" | custom-call | bytes 4718592 | tf_op jit(solution)/shard_map/pick_rows/pallas_call | solution.py:91
  12.6 6.9 %all-to-all-start.1 = ((bf16[8,48,2048]{2,1,0:T(8,128)(2,1)}), bf16[8,48,2048]{2,1,0:T(8,128)(2,1)S(1)}, u32[]{:S(2)}, u32[]{:S(2)}) async-start(bf16[8,48,2048]{2,1,0:T(8,128)(2,1)} %pick_rows.3), calls=%async_computation.1 | async-start | bytes 3145728 | tf_op jit(solution)/shard_map/all_to_all | solution.py:260
  19.5 3.4 %copy-done.1 = bf16[2,1024,2048]{2,1,0:T(8,128)(2,1)S(1)} copy-done((bf16[2,1024,2048]{2,1,0:T(8,128)(2,1)S(1)}, bf16[2,1024,2048]{2,1,0:T(8,128)(2,1)}, u32[]{:S(2)}) %copy-start.1) | copy-done | bytes 8388632
  22.9 2.2 %copy-done.3 = bf16[2,512,2048]{2,1,0:T(8,128)(2,1)S(1)} copy-done((bf16[2,512,2048]{2,1,0:T(8,128)(2,1)S(1)}, bf16[2,512,2048]{2,1,0:T(8,128)(2,1)}, u32[]{:S(2)}) %copy-start.3) | copy-done | bytes 4194328
  25.1 3.9 %pick_rows.2 = bf16[8,48,2048]{2,1,0:T(8,128)(2,1)S(1)} custom-call(s32[16]{0:T(128)S(1)} %copy-done.7, s32[8]{0:T(128)S(1)} %copy-done.9, s32[1]{0:T(128)} %bitcast.2.q_ref, bf16[2,512,2048]{2,1,0:T(8,128)(2,1)S(1)} %copy-done.3, bf16[2,1024,2048]{2,1,0:T(8,128)(2,1)S(1)} %copy-done.1), custom_call_target="tpu_custom_call" | custom-call | bytes 4718592 | tf_op jit(solution)/shard_map/pick_rows/pallas_call | solution.py:91
  29.0 1.1 copy-done.4
  30.2 9.9 %all-to-all-done.1.refs_0_ = bf16[8,48,2048]{2,1,0:T(8,128)(2,1)S(1)} async-done(((bf16[8,48,2048]{2,1,0:T(8,128)(2,1)}), bf16[8,48,2048]{2,1,0:T(8,128)(2,1)S(1)}, u32[]{:S(2)}, u32[]{:S(2)}) %all-to-all-start.1) | async-done | bytes 1572896 | tf_op jit(solution)/shard_map/all_to_all | solution.py:260
  40.0 3.7 %all-to-all-start = ((bf16[8,48,2048]{2,1,0:T(8,128)(2,1)}), bf16[8,48,2048]{2,1,0:T(8,128)(2,1)S(1)}, u32[]{:S(2)}, u32[]{:S(2)}) async-start(bf16[8,48,2048]{2,1,0:T(8,128)(2,1)} %copy-done.4), calls=%async_computation | async-start | bytes 3145728 | tf_op jit(solution)/shard_map/all_to_all | solution.py:260
  43.7 1.2 fusion
  45.0 1.2 collective-permute-start.5
  46.2 1.1 collective-permute-start.9
  47.2 1.5 collective-permute-start.6
  48.7 15.7 %all-to-all-done.refs_0_ = bf16[8,48,2048]{2,1,0:T(8,128)(2,1)S(1)} async-done(((bf16[8,48,2048]{2,1,0:T(8,128)(2,1)}), bf16[8,48,2048]{2,1,0:T(8,128)(2,1)S(1)}, u32[]{:S(2)}, u32[]{:S(2)}) %all-to-all-start) | async-done | bytes 1572896 | tf_op jit(solution)/shard_map/all_to_all | solution.py:260
  64.4 0.1 fusion.1
  64.5 1.2 collective-permute-start
  65.7 1.1 collective-permute-start.4
  66.8 1.5 collective-permute-start.1
  68.2 0.3 collective-permute-start.7
  68.5 15.7 %collective-permute-done.refs_0_ = bf16[4,48,2048]{2,1,0:T(8,128)(2,1)} collective-permute-done((bf16[4,48,2048]{2,1,0:T(8,128)(2,1)S(1)}, bf16[4,48,2048]{2,1,0:T(8,128)(2,1)}, u32[]{:S(2)}, u32[]{:S(2)}) %collective-permute-start) | collective-permute-done | bytes 786464 | tf_op jit(solution)/shard_map/ppermute | solution.py:261
  84.2 1.6 collective-permute-start.8
  85.8 0.2 collective-permute-done.1.refs_1_
  86.1 0.8 collective-permute-start.2
  86.8 0.1 pad_add_fusion.1.q_ref
  86.9 0.1 pad_add_fusion.q_ref
  87.0 23.2 %rotate_cast.4 = (bf16[128,16384]{1,0:T(8,128)(2,1)}, bf16[128,128]{1,0:T(8,128)(2,1)}, bf16[256,16384]{1,0:T(8,128)(2,1)}, bf16[256,128]{1,0:T(8,128)(2,1)}) custom-call(s32[2]{0:T(128)S(1)} %pad_add_fusion.1.q_ref, bf16[8,48,2048]{2,1,0:T(8,128)(2,1)S(1)} %all-to-all-done.1.refs_0_, bf16[8,48,2048]{2,1,0:T(8,128)(2,1)} %collective-permute-done.9.refs_1_, ...), custom_call_target="tpu_custom_call" | custom-call | flops 402653184 | bytes 6291456 | tf_op jit(solution)/shard_map/rotate_cast/pallas_call | solution.py:207
  110.2 23.4 %rotate_cast.5 = (bf16[128,16384]{1,0:T(8,128)(2,1)}, bf16[128,128]{1,0:T(8,128)(2,1)}, bf16[256,16384]{1,0:T(8,128)(2,1)}, bf16[256,128]{1,0:T(8,128)(2,1)}) custom-call(s32[2]{0:T(128)S(1)} %pad_add_fusion.q_ref, bf16[4,48,2048]{2,1,0:T(8,128)(2,1)} %collective-permute-done.5.refs_0_, ...), custom_call_target="tpu_custom_call", output_to_operand_aliasing={{0}: (6, {}), {1}: (7, {}), {2}: (8, {}), {3}: (9, {})} | custom-call | flops 402653184 | bytes 6291456 | tf_op jit(solution)/shard_map/rotate_cast/pallas_call | solution.py:207
  133.6 23.2 %rotate_cast.6 = (bf16[128,16384]{1,0:T(8,128)(2,1)}, bf16[128,128]{1,0:T(8,128)(2,1)}, bf16[256,16384]{1,0:T(8,128)(2,1)}, bf16[256,128]{1,0:T(8,128)(2,1)}) custom-call(s32[2]{0:T(128)S(1)} %pad_add_fusion.1.q_ref, bf16[8,48,2048]{2,1,0:T(8,128)(2,1)S(1)} %all-to-all-done.refs_0_, ...), custom_call_target="tpu_custom_call", output_to_operand_aliasing={{0}: (4, {}), {1}: (5, {}), {2}: (6, {}), {3}: (7, {})} | custom-call | flops 402653184 | bytes 6291456 | tf_op jit(solution)/shard_map/rotate_cast/pallas_call | solution.py:207
  156.8 23.4 %rotate_cast.7 = (bf16[128,16384]{1,0:T(8,128)(2,1)}, bf16[128,128]{1,0:T(8,128)(2,1)}, bf16[256,16384]{1,0:T(8,128)(2,1)}, bf16[256,128]{1,0:T(8,128)(2,1)}) custom-call(s32[2]{0:T(128)S(1)} %pad_add_fusion.q_ref, bf16[4,48,2048]{2,1,0:T(8,128)(2,1)} %collective-permute-done.refs_0_, ...), custom_call_target="tpu_custom_call", output_to_operand_aliasing={{0}: (6, {}), {1}: (7, {}), {2}: (8, {}), {3}: (9, {})} | custom-call | flops 402653184 | bytes 6291456 | tf_op jit(solution)/shard_map/rotate_cast/pallas_call | solution.py:207
  (22 shorter events, 0.1 us)
Async XLA Ops:
  0.6 3.4 %copy-start = (bf16[2,1024,2048]{2,1,0:T(8,128)(2,1)S(1)}, bf16[2,1024,2048]{2,1,0:T(8,128)(2,1)}, u32[]{:S(2)}) copy-start(bf16[2,1024,2048]{2,1,0:T(8,128)(2,1)} %down_hbm.3) | copy-start | bytes 25165828
  4.0 2.2 %copy-start.2 = (bf16[2,512,2048]{2,1,0:T(8,128)(2,1)S(1)}, bf16[2,512,2048]{2,1,0:T(8,128)(2,1)}, u32[]{:S(2)}) copy-start(bf16[2,512,2048]{2,1,0:T(8,128)(2,1)} %out_hbm.3) | copy-start | bytes 12582916
  6.2 0.7 copy-start.6
  6.9 0.7 copy-start.8
  7.5 12.0 %copy-start.7 = (s32[16]{0:T(128)S(1)}, s32[16]{0:T(128)}, u32[]{:S(2)}) copy-start(s32[16]{0:T(128)} %share.3) | copy-start | bytes 196
  7.5 12.0 %copy-start.9 = (s32[8]{0:T(128)S(1)}, s32[8]{0:T(128)}, u32[]{:S(2)}) copy-start(s32[8]{0:T(128)} %ranks.3) | copy-start | bytes 100
  12.6 27.4 %all-to-all-start.1 = ((bf16[8,48,2048]{2,1,0:T(8,128)(2,1)}), bf16[8,48,2048]{2,1,0:T(8,128)(2,1)S(1)}, u32[]{:S(2)}, u32[]{:S(2)}) async-start(bf16[8,48,2048]{2,1,0:T(8,128)(2,1)} %pick_rows.3), calls=%async_computation.1 | async-start | bytes 3145728 | tf_op jit(solution)/shard_map/all_to_all | solution.py:260
  19.5 3.4 %copy-start.1 = (bf16[2,1024,2048]{2,1,0:T(8,128)(2,1)S(1)}, bf16[2,1024,2048]{2,1,0:T(8,128)(2,1)}, u32[]{:S(2)}) copy-start(bf16[2,1024,2048]{2,1,0:T(8,128)(2,1)} %down_hbm.3) | copy-start | bytes 25165828
  22.9 2.2 %copy-start.3 = (bf16[2,512,2048]{2,1,0:T(8,128)(2,1)S(1)}, bf16[2,512,2048]{2,1,0:T(8,128)(2,1)}, u32[]{:S(2)}) copy-start(bf16[2,512,2048]{2,1,0:T(8,128)(2,1)} %out_hbm.3) | copy-start | bytes 12582916
  29.0 1.1 copy-start.4
  30.2 56.8 %copy-start.5 = (bf16[256,256]{1,0:T(8,128)(2,1)S(1)}, bf16[256,256]{1,0:T(8,128)(2,1)}, u32[]{:S(2)}) copy-start(bf16[256,256]{1,0:T(8,128)(2,1)} %constant.24.clone.refs_2_.refs_4_) | copy-start | bytes 393220
  40.0 24.4 %all-to-all-start = ((bf16[8,48,2048]{2,1,0:T(8,128)(2,1)}), bf16[8,48,2048]{2,1,0:T(8,128)(2,1)S(1)}, u32[]{:S(2)}, u32[]{:S(2)}) async-start(bf16[8,48,2048]{2,1,0:T(8,128)(2,1)} %copy-done.4), calls=%async_computation | async-start | bytes 3145728 | tf_op jit(solution)/shard_map/all_to_all | solution.py:260
  45.0 21.8 %collective-permute-start.5 = (bf16[4,48,2048]{2,1,0:T(8,128)(2,1)}, bf16[4,48,2048]{2,1,0:T(8,128)(2,1)}, u32[]{:S(2)}, u32[]{:S(2)}) collective-permute-start(bf16[4,48,2048]{2,1,0:T(8,128)(2,1)} %get-tuple-element.37), channel_id=1, source_target_pairs={{0,2},{1,3},{2,4},{3,5},{4,6},{5,7},{6,0},{7,1},{8,10},{9,11},{10,... | collective-permute-start | bytes 2359304 | tf_op jit(solution)/shard_map/ppermute | solution.py:261
  46.2 40.7 %collective-permute-start.9 = (bf16[8,48,2048]{2,1,0:T(8,128)(2,1)S(1)}, bf16[8,48,2048]{2,1,0:T(8,128)(2,1)}, u32[]{:S(2)}, u32[]{:S(2)}) collective-permute-start(bf16[8,48,2048]{2,1,0:T(8,128)(2,1)S(1)} %all-to-all-done.1.refs_0_), channel_id=1, source_target_pairs={{0,1},{1,0},{2,3},{3,2},{4,5},{5,4},{6,7},{7,6},{8,9},{9,8},{10,11... | collective-permute-start | bytes 4718600 | tf_op jit(solution)/shard_map/ppermute | solution.py:263
  47.2 21.0 %collective-permute-start.6 = (bf16[4,48,2048]{2,1,0:T(8,128)(2,1)}, bf16[4,48,2048]{2,1,0:T(8,128)(2,1)}, u32[]{:S(2)}, u32[]{:S(2)}) collective-permute-start(bf16[4,48,2048]{2,1,0:T(8,128)(2,1)} %get-tuple-element.36), channel_id=1, source_target_pairs={{0,6},{1,7},{2,0},{3,1},{4,2},{5,3},{6,4},{7,5},{8,14},{9,15},{10,... | collective-permute-start | bytes 2359304 | tf_op jit(solution)/shard_map/ppermute | solution.py:262
  64.5 19.7 %collective-permute-start = (bf16[4,48,2048]{2,1,0:T(8,128)(2,1)S(1)}, bf16[4,48,2048]{2,1,0:T(8,128)(2,1)}, u32[]{:S(2)}, u32[]{:S(2)}) collective-permute-start(bf16[4,48,2048]{2,1,0:T(8,128)(2,1)S(1)} %get-tuple-element.39), channel_id=1, source_target_pairs={{0,2},{1,3},{2,4},{3,5},{4,6},{5,7},{6,0},{7,1},{8,10},{9,11},{10,... | collective-permute-start | bytes 2359304 | tf_op jit(solution)/shard_map/ppermute | solution.py:261
  65.7 67.9 %collective-permute-start.4 = (bf16[8,48,2048]{2,1,0:T(8,128)(2,1)S(1)}, bf16[8,48,2048]{2,1,0:T(8,128)(2,1)}, u32[]{:S(2)}, u32[]{:S(2)}) collective-permute-start(bf16[8,48,2048]{2,1,0:T(8,128)(2,1)S(1)} %all-to-all-done.refs_0_), channel_id=1, source_target_pairs={{0,1},{1,0},{2,3},{3,2},{4,5},{5,4},{6,7},{7,6},{8,9},{9,8},{10,11... | collective-permute-start | bytes 4718600 | tf_op jit(solution)/shard_map/ppermute | solution.py:263
  66.8 19.3 %collective-permute-start.1 = (bf16[4,48,2048]{2,1,0:T(8,128)(2,1)S(1)}, bf16[4,48,2048]{2,1,0:T(8,128)(2,1)}, u32[]{:S(2)}, u32[]{:S(2)}) collective-permute-start(bf16[4,48,2048]{2,1,0:T(8,128)(2,1)S(1)} %get-tuple-element.38), channel_id=1, source_target_pairs={{0,6},{1,7},{2,0},{3,1},{4,2},{5,3},{6,4},{7,5},{8,14},{9,15},{10,... | collective-permute-start | bytes 2359304 | tf_op jit(solution)/shard_map/ppermute | solution.py:262
  68.2 42.0 %collective-permute-start.7 = (bf16[4,48,2048]{2,1,0:T(8,128)(2,1)}, bf16[4,48,2048]{2,1,0:T(8,128)(2,1)}, u32[]{:S(2)}, u32[]{:S(2)}) collective-permute-start(bf16[4,48,2048]{2,1,0:T(8,128)(2,1)} %collective-permute-done.5.refs_0_), channel_id=1, source_target_pairs={{0,1},{1,0},{2,3},{3,2},{4,5},{5,4},{6,7},{7,6},{8,9},{9,8},{10,11... | collective-permute-start | bytes 2359304 | tf_op jit(solution)/shard_map/ppermute | solution.py:264
  84.2 26.0 %collective-permute-start.8 = (bf16[4,48,2048]{2,1,0:T(8,128)(2,1)}, bf16[4,48,2048]{2,1,0:T(8,128)(2,1)}, u32[]{:S(2)}, u32[]{:S(2)}) collective-permute-start(bf16[4,48,2048]{2,1,0:T(8,128)(2,1)} %collective-permute-done.6.refs_1_), channel_id=1, source_target_pairs={{0,1},{1,0},{2,3},{3,2},{4,5},{5,4},{6,7},{7,6},{8,9},{9,8},{10,11... | collective-permute-start | bytes 2359304 | tf_op jit(solution)/shard_map/ppermute | solution.py:265
  86.1 70.8 %collective-permute-start.2 = (bf16[4,48,2048]{2,1,0:T(8,128)(2,1)}, bf16[4,48,2048]{2,1,0:T(8,128)(2,1)}, u32[]{:S(2)}, u32[]{:S(2)}) collective-permute-start(bf16[4,48,2048]{2,1,0:T(8,128)(2,1)} %collective-permute-done.refs_0_), channel_id=1, source_target_pairs={{0,1},{1,0},{2,3},{3,2},{4,5},{5,4},{6,7},{7,6},{8,9},{9,8},{10,11... | collective-permute-start | bytes 2359304 | tf_op jit(solution)/shard_map/ppermute | solution.py:264
  86.8 70.0 %collective-permute-start.3 = (bf16[4,48,2048]{2,1,0:T(8,128)(2,1)}, bf16[4,48,2048]{2,1,0:T(8,128)(2,1)}, u32[]{:S(2)}, u32[]{:S(2)}) collective-permute-start(bf16[4,48,2048]{2,1,0:T(8,128)(2,1)} %collective-permute-done.1.refs_1_), channel_id=1, source_target_pairs={{0,1},{1,0},{2,3},{3,2},{4,5},{5,4},{6,7},{7,6},{8,9},{9,8},{10,11... | collective-permute-start | bytes 2359304 | tf_op jit(solution)/shard_map/ppermute | solution.py:265

commit v2 on v1

v2 whole, which is shorter than its diff:
```python
import functools
import math

import jax
import jax.numpy as jnp
import numpy as np
from jax import lax
from jax.experimental import pallas as pl
from jax.experimental.pallas import tpu as pltpu
from jax.sharding import PartitionSpec as P

SIDE = 128
UNIT = 16
LOCAL = 2048
BLOCKS = LOCAL // SIDE
SHARDS = 8
PARTS = ((0, 0, 0, 3), (0, 2, 3, 0), (2, 0, 3, 1))
VMEM = 60 * 2**20


def signs(order):
    h = np.ones((1, 1), np.float32)
    while h.shape[0] < order:
        h = np.block([[h, h], [h, -h]])
    return h


def two_blocks():
    h = signs(SIDE)
    z = np.zeros_like(h)
    return jnp.asarray(np.block([[h, z], [z, h]]) / SIDE, jnp.bfloat16)


def butterflies(values):
    span = 1
    values = list(values)
    while span < len(values):
        for i in range(len(values)):
            if i & span == 0:
                lo, hi = values[i], values[i + span]
                values[i], values[i + span] = lo + hi, lo - hi
        span *= 2
    return values


def pick_kernel(part, share, ranks, q_ref, out_hbm, down_hbm, send, pairs, stage, sems, gone):
    o0, no, d0, nd = part
    q = q_ref[0]
    n = 2 * no + nd
    copies = []
    for f in range(SHARDS):
        mine = []
        for u in range(no):
            for h in range(2):
                block = share[4 * q + 2 * (o0 + u) + h]
                row = ranks[f] * 64 + lax.rem(block, 8) // 2 * 16
                mine.append(
                    pltpu.make_async_copy(
                        out_hbm.at[block // 8, pl.ds(pl.multiple_of(row, 16), 16), :],
                        pairs.at[u, h, f],
                        sems.at[f * n + len(mine)],
                    )
                )
        for u in range(nd):
            block = share[4 * q + d0 + u]
            row = ranks[f] * 128 + lax.rem(block, 8) * 16
            mine.append(
                pltpu.make_async_copy(
                    down_hbm.at[block // 8, pl.ds(pl.multiple_of(row, 16), 16), :],
                    stage.at[f, pl.ds((no + u) * UNIT, UNIT), :],
                    sems.at[f * n + len(mine)],
                )
            )
        for c in mine:
            c.start()
        copies.append(mine)
    odd = [
        [lax.rem(share[4 * q + 2 * (o0 + u) + h], 2) == 1 for h in range(2)]
        for u in range(no)
    ]
    leaving = []
    for f in range(SHARDS):
        for c in copies[f]:
            c.wait()
        for u in range(no):
            halves = []
            for h in range(2):
                rows = pairs[u, h, f].astype(jnp.float32)
                halves.append(jnp.where(odd[u][h], rows[8:], rows[:8]))
            stage[f, pl.ds(u * UNIT, UNIT), :] = jnp.concatenate(halves, 0).astype(
                jnp.bfloat16
            )
        c = pltpu.make_async_copy(stage.at[f], send.at[f], gone.at[f])
        c.start()
        leaving.append(c)
    for c in leaving:
        c.wait()


def pick(part, share, ranks, q, out_weight, down_weight):
    o0, no, d0, nd = part
    n = (no * 2 + nd) * SHARDS
    shape = (SHARDS, (no + nd) * UNIT, LOCAL)
    return pl.pallas_call(
        functools.partial(pick_kernel, part),
        grid_spec=pltpu.PrefetchScalarGridSpec(
            num_scalar_prefetch=3,
            grid=(),
            in_specs=[pl.BlockSpec(memory_space=pltpu.HBM)] * 2,
            out_specs=pl.BlockSpec(memory_space=pltpu.HBM),
            scratch_shapes=[
                pltpu.VMEM((max(no, 1), 2, SHARDS, UNIT, LOCAL), jnp.bfloat16),
                pltpu.VMEM(shape, jnp.bfloat16),
                pltpu.SemaphoreType.DMA((n,)),
                pltpu.SemaphoreType.DMA((SHARDS,)),
            ],
        ),
        out_shape=jax.ShapeDtypeStruct(shape, jnp.bfloat16),
        compiler_params=pltpu.CompilerParams(vmem_limit_bytes=VMEM),
        cost_estimate=pl.CostEstimate(
            flops=0, bytes_accessed=3 * math.prod(shape) * 2, transcendentals=0
        ),
        name="pick_rows",
    )(share, ranks, q, out_weight, down_weight)


def spread(refs, rot, work):
    first = 0
    for ref in refs:
        for s in range(ref.shape[0]):
            x = ref[s]
            stack = jnp.concatenate(
                [x[:, c * 256 : (c + 1) * 256] for c in range(BLOCKS // 2)], 0
            )
            y = jnp.dot(stack, rot, preferred_element_type=jnp.float32)
            parts = butterflies(
                y[c * UNIT : (c + 1) * UNIT, h * SIDE : (h + 1) * SIDE]
                for c in range(BLOCKS // 2)
                for h in range(2)
            )
            for k in range(BLOCKS):
                work[first + k] = parts[k]
            first += BLOCKS


def finish(quant, scales, work):
    lane = lax.broadcasted_iota(jnp.int32, (UNIT, SIDE), 1)
    top = jnp.zeros((UNIT, SIDE), jnp.float32)
    for k in range(BLOCKS):
        parts = butterflies(work[f * BLOCKS + k] for f in range(SHARDS))
        for f in range(SHARDS):
            a = f * BLOCKS + k
            m = jnp.max(jnp.abs(parts[f]), axis=1, keepdims=True)
            s = (m + 1e-06).astype(jnp.bfloat16).astype(jnp.float32)
            quant[:, a * SIDE : (a + 1) * SIDE] = (parts[f] * (1.0 / s)).astype(
                jnp.bfloat16
            )
            top = jnp.where(lane == a, m, top)
    scales[...] = (top + 1e-06).astype(jnp.bfloat16)


def rotate_kernel(counts, no, nd, n_alias, q_ref, *refs):
    groups, at = [], 0
    for n in counts:
        groups.append(refs[at : at + n])
        at += n
    rot_ref = refs[at]
    at += 1 + n_alias
    work = refs[-1]
    outs = list(refs[at:-1])
    u, g = pl.program_id(0), pl.program_id(1)
    for i, group in enumerate(groups):

        @pl.when(g == i)
        def _(group=group):
            spread(group, rot_ref[...], work)

    if no:

        @pl.when(u < no)
        def _(quant=outs.pop(0), scales=outs.pop(0)):
            finish(quant, scales, work)

    if nd:

        @pl.when(u >= no)
        def _(quant=outs.pop(0), scales=outs.pop(0)):
            finish(quant, scales, work)


def rotate(part, groups, q_here, flips, rot, before):
    o0, no, d0, nd = part
    n_groups = len(groups)
    flat = [b for group in groups for b in group]

    def sharer(q, g):
        return q[0] ^ (flips[0] + g)

    def out_at(u, g, q):
        last = u >= no
        g = jnp.where(last, n_groups - 1, g)
        return 2 * sharer(q, g) + o0 + jnp.where(last, no - 1, u), 0

    def down_at(u, g, q):
        early = u < no
        g = jnp.where(early, 0, g)
        return 4 * sharer(q, g) + d0 + jnp.where(early, 0, u - no), 0

    in_specs = [
        pl.BlockSpec((b.shape[0], UNIT, LOCAL), lambda u, g, q: (0, u, 0)) for b in flat
    ]
    in_specs.append(pl.BlockSpec((256, 256), lambda u, g, q: (0, 0)))
    operands = flat + [rot]
    columns = SHARDS * LOCAL
    shapes = [(128, columns), (128, SIDE), (256, columns), (256, SIDE)]
    maps = [out_at, out_at, down_at, down_at]
    used = [i for i in range(4) if (no, no, nd, nd)[i]]
    aliases = {}
    for i, t in enumerate(used):
        if before[t] is not None:
            aliases[1 + len(operands)] = i
            operands.append(before[t])
            in_specs.append(pl.BlockSpec(memory_space=pltpu.HBM))
    elements = n_groups * (no + nd) * UNIT * columns
    results = pl.pallas_call(
        functools.partial(
            rotate_kernel, [len(g) for g in groups], no, nd, len(aliases)
        ),
        grid_spec=pltpu.PrefetchScalarGridSpec(
            num_scalar_prefetch=1,
            grid=(no + nd, n_groups),
            in_specs=in_specs,
            out_specs=[pl.BlockSpec((UNIT, shapes[t][1]), maps[t]) for t in used],
            scratch_shapes=[
                pltpu.VMEM((SHARDS * BLOCKS, UNIT, SIDE), jnp.float32)
            ],
        ),
        out_shape=[jax.ShapeDtypeStruct(shapes[t], jnp.bfloat16) for t in used],
        input_output_aliases=aliases,
        compiler_params=pltpu.CompilerParams(vmem_limit_bytes=VMEM),
        cost_estimate=pl.CostEstimate(
            flops=elements * 256, bytes_accessed=elements * 4, transcendentals=0
        ),
        name="rotate_cast",
    )(q_here, *operands)
    after = list(before)
    for t, r in zip(used, results):
        after[t] = r
    return after


def replica_steps(step):
    pairs = []
    for y in range(2):
        for x in range(4):
            for c in range(2):
                y2, x2, c2 = step(y, x, c)
                pairs.append(((y * 4 + x) * 2 + c, (y2 * 4 + x2 % 4) * 2 + c2))
    return pairs


ALONG = replica_steps(lambda y, x, c: (y, x + 1 + 2 * c, c))
OTHER = replica_steps(lambda y, x, c: (y, x, 1 - c))


def shards(out_weight, down_weight, layer_share, rank_map):
    here = lax.axis_index("replica")
    q = (here % 4).astype(jnp.int32)[None]
    rot = two_blocks()
    sends = [
        pick(part, layer_share, rank_map, q, out_weight, down_weight)
        for part in PARTS
    ]
    def swap(value):
        return lax.ppermute(value, "replica", OTHER)

    def exchange(own):
        return swap(own), lax.ppermute(own, "replica", ALONG)

    def to_owner(send):
        return lax.all_to_all(send, "fsdp", split_axis=0, concat_axis=0, tiled=True)

    def near(k, own, other, done):
        return rotate(PARTS[k], [[own], [other]], q, (0, 1), rot, done)

    def far(k, along, along_other, done):
        return rotate(PARTS[k], [[along], [along_other]], q, (2, 3), rot, done)

    def tied(value, *others):
        return lax.optimization_barrier((value,) + others)

    done = [None] * 4
    own0 = to_owner(sends[0])
    send1, own0 = tied(sends[1], own0)
    other0, along0 = exchange(own0)
    along_other0 = swap(along0)
    own1 = to_owner(send1)
    done = near(0, own0, other0, done)
    send2, own1, done[2] = tied(sends[2], own1, done[2])
    other1, along1 = exchange(own1)
    along_other1 = swap(along1)
    own2 = to_owner(send2)
    done = near(1, own1, other1, done)
    own2, done[0] = tied(own2, done[0])
    other2, along2 = exchange(own2)
    done = far(0, along0, along_other0, done)
    along2, done[2] = tied(along2, done[2])
    along_other2 = swap(along2)
    done = near(2, own2, other2, done)
    done = far(1, along1, along_other1, done)
    done = far(2, along2, along_other2, done)
    return tuple(d[None] for d in done)


def solution(mesh):
    return jax.shard_map(
        shards,
        mesh=mesh,
        in_specs=(P(None, None, "fsdp"), P(None, None, "fsdp"), P(), P()),
        out_specs=(P("fsdp", None, None),) * 4,
        check_vma=False,
    )
```

time: 181 us -> 103 us (0.57)
  Pallas kernels: 102 us -> 43.8 us
  local copies, waits for them, and re-layouts: 14.9 us -> 1.83 us
  waiting for transfers between devices: 41.5 us -> 31.8 us
  starting transfers between devices: 20.7 us -> 23.7 us
    pallas_call x4 -> x6, Pallas kernels: 93.2 us -> 34.8 us  [rotate(): pl.pallas_call(functools.partial(rotate_kernel, [len(g) for g in groups],...]
    unnamed x20 -> x14, local copies, waits for them, and re-layouts: 13.6 us -> 1.83 us
    all_to_all x2 -> x3, waiting for transfers between devices: 25.5 us -> 20.7 us  [to_owner(): return lax.all_to_all(send, 'fsdp', split_axis=0, concat_axis=0, tiled=True)]
    ppermute x10 -> x9, waiting for transfers between devices: 15.9 us -> 11.1 us  [the longest x3 11.1 us: exchange(): return (swap(own), lax.ppermute(own, 'replica', ALONG))]
    all_to_all x2 -> x3, starting transfers between devices: 10.6 us -> 14.1 us  [to_owner(): return lax.all_to_all(send, 'fsdp', split_axis=0, concat_axis=0, tiled=True)]
    ppermute x10 -> x9, starting transfers between devices: 10.1 us -> 9.61 us  [the longest x6 5.8 us: swap(): return lax.ppermute(value, 'replica', OTHER)]
    pallas_call x2 -> x3, Pallas kernels: 8.99 us -> 9.02 us  [pick(): pl.pallas_call(functools.partial(pick_kernel, part), grid_spec=pltpu.Pref...]
  transfers between devices with their start and end apart: 12 -> 12, of which waited for: 4 -> 3; matrix products, arithmetic and copies ran while one was open for 1% -> 0% of each run, Pallas kernels for 41% -> 34%
where the time goes in v2:
time: 103 us; the launch traced here: 102 us
  Pallas kernels  43.8 us (43%)
  waiting for transfers between devices  31.8 us (31%)
  starting transfers between devices  23.7 us (23%)
  local copies, waits for them, and re-layouts  1.83 us (2%)
    pallas_call x6, Pallas kernels, rotate(): pl.pallas_call(functools.partial(rotate_kernel, [len(g) for g in groups],...  34.8 us
    all_to_all x3, waiting for transfers between devices, to_owner(): return lax.all_to_all(send, 'fsdp', split_axis=0, concat_axis=0, tiled=True)  20.7 us
    all_to_all x3, starting transfers between devices, to_owner(): return lax.all_to_all(send, 'fsdp', split_axis=0, concat_axis=0, tiled=True)  14.1 us
    ppermute x3, waiting for transfers between devices, exchange(): return (swap(own), lax.ppermute(own, 'replica', ALONG))  11.1 us
    pallas_call x3, Pallas kernels, pick(): pl.pallas_call(functools.partial(pick_kernel, part), grid_spec=pltpu.Pref...  9.02 us
    ppermute x6, starting transfers between devices, swap(): return lax.ppermute(value, 'replica', OTHER)  5.8 us
    ppermute x3, starting transfers between devices, exchange(): return (swap(own), lax.ppermute(own, 'replica', ALONG))  3.81 us
  transfers between devices with their start and end apart: 12, of which 3 were waited for; matrix products, arithmetic and copies ran while one was open for 0% of the time, Pallas kernels for 34%

profile of v2, /device:TPU:1, one launch (start us, length us, event | category | flops | bytes accessed | tf_op | source)
XLA Modules:
  0.0 101.9 jit_solution(5994301834843567874)
XLA Ops:
  0.6 3.1 %pick_rows.5 = bf16[8,48,2048]{2,1,0:T(8,128)(2,1)} custom-call(s32[16]{0:T(128)} %share.5, s32[8]{0:T(128)} %ranks.5, s32[1]{0:T(128)} %bitcast.q_ref, bf16[2,512,2048]{2,1,0:T(8,128)(2,1)} %out_hbm.5, bf16[2,1024,2048]{2,1,0:T(8,128)(2,1)} %down_hbm.5), custom_call_target="tpu_custom_call" | custom-call | bytes 4718592 | tf_op jit(solution)/shard_map/pick_rows/pallas_call | solution.py:104
  3.7 6.9 %all-to-all-start = ((bf16[8,48,2048]{2,1,0:T(8,128)(2,1)}), bf16[8,48,2048]{2,1,0:T(8,128)(2,1)S(1)}, u32[]{:S(2)}, u32[]{:S(2)}) async-start(bf16[8,48,2048]{2,1,0:T(8,128)(2,1)} %pick_rows.5), calls=%async_computation | async-start | bytes 3145728 | tf_op jit(solution)/shard_map/all_to_all | solution.py:281
  10.6 3.4 %pick_rows.4 = bf16[8,32,2048]{2,1,0:T(8,128)(2,1)} custom-call(s32[16]{0:T(128)} %share.5, s32[8]{0:T(128)} %ranks.5, s32[1]{0:T(128)} %bitcast.q_ref, bf16[2,512,2048]{2,1,0:T(8,128)(2,1)} %out_hbm.5, bf16[2,1024,2048]{2,1,0:T(8,128)(2,1)} %down_hbm.5), custom_call_target="tpu_custom_call" | custom-call | bytes 3145728 | tf_op jit(solution)/shard_map/pick_rows/pallas_call | solution.py:104
  14.1 17.1 %all-to-all-done.refs_0_ = bf16[8,48,2048]{2,1,0:T(8,128)(2,1)S(1)} async-done(((bf16[8,48,2048]{2,1,0:T(8,128)(2,1)}), bf16[8,48,2048]{2,1,0:T(8,128)(2,1)S(1)}, u32[]{:S(2)}, u32[]{:S(2)}) %all-to-all-start) | async-done | bytes 1572896 | tf_op jit(solution)/shard_map/all_to_all | solution.py:281
  31.1 2.5 %collective-permute-start.5 = (bf16[8,48,2048]{2,1,0:T(8,128)(2,1)S(1)}, bf16[8,48,2048]{2,1,0:T(8,128)(2,1)}, u32[]{:S(2)}, u32[]{:S(2)}) collective-permute-start(bf16[8,48,2048]{2,1,0:T(8,128)(2,1)S(1)} %all-to-all-done.refs_0_), channel_id=1, source_target_pairs={{0,2},{1,7},{2,4},{3,1},{4,6},{5,3},{6,0},{7,5},{8,10},{9,15},{10,... | collective-permute-start | bytes 4718600 | tf_op jit(solution)/shard_map/ppermute | solution.py:278
  33.6 0.0 collective-permute-start
  33.6 3.7 %all-to-all-start.1 = ((bf16[8,32,2048]{2,1,0:T(8,128)(2,1)}), bf16[8,32,2048]{2,1,0:T(8,128)(2,1)S(1)}, u32[]{:S(2)}, u32[]{:S(2)}) async-start(bf16[8,32,2048]{2,1,0:T(8,128)(2,1)} %pick_rows.4), calls=%async_computation.1 | async-start | bytes 2097152 | tf_op jit(solution)/shard_map/all_to_all | solution.py:281
  37.3 2.5 %pick_rows.3 = bf16[8,16,2048]{2,1,0:T(8,128)(2,1)} custom-call(s32[16]{0:T(128)} %share.5, s32[8]{0:T(128)} %ranks.5, s32[1]{0:T(128)} %bitcast.q_ref, bf16[2,512,2048]{2,1,0:T(8,128)(2,1)} %out_hbm.5, bf16[2,1024,2048]{2,1,0:T(8,128)(2,1)} %down_hbm.5), custom_call_target="tpu_custom_call" | custom-call | bytes 1572864 | tf_op jit(solution)/shard_map/pick_rows/pallas_call | solution.py:104
  39.9 11.1 %collective-permute-done.5.refs_0_ = bf16[8,48,2048]{2,1,0:T(8,128)(2,1)} collective-permute-done((bf16[8,48,2048]{2,1,0:T(8,128)(2,1)S(1)}, bf16[8,48,2048]{2,1,0:T(8,128)(2,1)}, u32[]{:S(2)}, u32[]{:S(2)}) %collective-permute-start.5) | collective-permute-done | bytes 1572896 | tf_op jit(solution)/shard_map/ppermute | solution.py:278
  51.0 2.7 %collective-permute-start.6 = (bf16[8,48,2048]{2,1,0:T(8,128)(2,1)}, bf16[8,48,2048]{2,1,0:T(8,128)(2,1)}, u32[]{:S(2)}, u32[]{:S(2)}) collective-permute-start(bf16[8,48,2048]{2,1,0:T(8,128)(2,1)} %collective-permute-done.5.refs_0_), channel_id=1, source_target_pairs={{0,1},{1,0},{2,3},{3,2},{4,5},{5,4},{6,7},{7,6},{8,9},{9,8},{10,11... | collective-permute-start | bytes 4718600 | tf_op jit(solution)/shard_map/ppermute | solution.py:275
  53.7 0.0 collective-permute-done.refs_1_
  53.7 8.0 %rotate_cast.6 = (bf16[256,16384]{1,0:T(8,128)(2,1)}, bf16[256,128]{1,0:T(8,128)(2,1)}) custom-call(s32[1]{0:T(128)} %bitcast.q_ref, bf16[8,48,2048]{2,1,0:T(8,128)(2,1)} %copy-done, bf16[8,48,2048]{2,1,0:T(8,128)(2,1)} %collective-permute-done.refs_1_, bf16[256,256]{1,0:T(8,128)(2,1)} %constant.19.clone.refs_2_), custom_call_target="tpu_custom_call" | custom-call | flops 402653184 | bytes 6291456 | tf_op jit(solution)/shard_map/rotate_cast/pallas_call | solution.py:225
  61.7 0.0 all-to-all-done.1.refs_0_
  61.8 0.1 collective-permute-start.3
  61.8 1.3 %collective-permute-start.1 = (bf16[8,32,2048]{2,1,0:T(8,128)(2,1)S(1)}, bf16[8,32,2048]{2,1,0:T(8,128)(2,1)S(1)}, u32[]{:S(2)}, u32[]{:S(2)}) collective-permute-start(bf16[8,32,2048]{2,1,0:T(8,128)(2,1)S(1)} %all-to-all-done.1.refs_0_), channel_id=1, source_target_pairs={{0,2},{1,7},{2,4},{3,1},{4,6},{5,3},{6,0},{7,5},{8,10},{9,15},{10,... | collective-permute-start | bytes 3145736 | tf_op jit(solution)/shard_map/ppermute | solution.py:278
  63.2 3.5 %all-to-all-start.2 = ((bf16[8,16,2048]{2,1,0:T(8,128)(2,1)}), bf16[8,16,2048]{2,1,0:T(8,128)(2,1)S(1)}, u32[]{:S(2)}, u32[]{:S(2)}) async-start(bf16[8,16,2048]{2,1,0:T(8,128)(2,1)} %pick_rows.3), calls=%async_computation.2 | async-start | bytes 1048576 | tf_op jit(solution)/shard_map/all_to_all | solution.py:281
  66.7 0.0 collective-permute-done.3.refs_1_
  66.7 5.8 %rotate_cast.7 = (bf16[128,16384]{1,0:T(8,128)(2,1)}, bf16[128,128]{1,0:T(8,128)(2,1)}) custom-call(s32[1]{0:T(128)} %bitcast.q_ref, bf16[8,32,2048]{2,1,0:T(8,128)(2,1)} %copy-done.1, bf16[8,32,2048]{2,1,0:T(8,128)(2,1)} %collective-permute-done.3.refs_1_, bf16[256,256]{1,0:T(8,128)(2,1)} %constant.19.clone.refs_2_), custom_call_target="tpu_custom_call" | custom-call | flops 268435456 | bytes 4194304 | tf_op jit(solution)/shard_map/rotate_cast/pallas_call | solution.py:225
  72.5 3.6 %all-to-all-done.2.refs_0_ = bf16[8,16,2048]{2,1,0:T(8,128)(2,1)S(1)} async-done(((bf16[8,16,2048]{2,1,0:T(8,128)(2,1)}), bf16[8,16,2048]{2,1,0:T(8,128)(2,1)S(1)}, u32[]{:S(2)}, u32[]{:S(2)}) %all-to-all-start.2) | async-done | bytes 524320 | tf_op jit(solution)/shard_map/all_to_all | solution.py:281
  76.1 0.0 collective-permute-start.4
  76.1 0.0 collective-permute-done.1.refs_0_
  76.1 2.2 %collective-permute-start.2 = (bf16[8,32,2048]{2,1,0:T(8,128)(2,1)S(1)}, bf16[8,32,2048]{2,1,0:T(8,128)(2,1)S(1)}, u32[]{:S(2)}, u32[]{:S(2)}) collective-permute-start(bf16[8,32,2048]{2,1,0:T(8,128)(2,1)S(1)} %collective-permute-done.1.refs_0_), channel_id=1, source_target_pairs={{0,1},{1,0},{2,3},{3,2},{4,5},{5,4},{6,7},{7,6},{8,9},{9,8},{10,11... | collective-permute-start | bytes 3145736 | tf_op jit(solution)/shard_map/ppermute | solution.py:275
  78.4 0.0 collective-permute-start.8
  78.4 0.0 collective-permute-done.6.refs_1_
  78.4 8.0 %rotate_cast.9 = (bf16[256,16384]{1,0:T(8,128)(2,1)}, bf16[256,128]{1,0:T(8,128)(2,1)}) custom-call(s32[1]{0:T(128)} %bitcast.q_ref, bf16[8,48,2048]{2,1,0:T(8,128)(2,1)} %collective-permute-done.5.refs_0_, bf16[8,48,2048]{2,1,0:T(8,128)(2,1)} %collective-permute-done.6.refs_1_, ...), custom_call_target="tpu_custom_call", output_to_operand_aliasing={{0}: (4, {}), {1}: (5, {})} | custom-call | flops 402653184 | bytes 6291456 | tf_op jit(solution)/shard_map/rotate_cast/pallas_call | solution.py:225
  86.4 0.0 collective-permute-done.4.refs_0_
  86.4 0.7 collective-permute-start.7
  87.1 0.8 copy-done.6
  87.9 3.6 %rotate_cast.10 = (bf16[256,16384]{1,0:T(8,128)(2,1)}, bf16[256,128]{1,0:T(8,128)(2,1)}) custom-call(s32[1]{0:T(128)} %bitcast.q_ref, bf16[8,16,2048]{2,1,0:T(8,128)(2,1)} %copy-done.2, bf16[8,16,2048]{2,1,0:T(8,128)(2,1)} %copy-done.6, bf16[256,256]{1,0:T(8,128)(2,1)} %constant.19.clone.refs_2_, ...), custom_call_target="tpu_custom_call", output_to_operand_aliasing={{0}: (4, {}), {1}: (5, {})} | custom-call | flops 134217728 | bytes 2097152 | tf_op jit(solution)/shard_map/rotate_cast/pallas_call | solution.py:225
  91.5 3.6 %rotate_cast.11 = (bf16[256,16384]{1,0:T(8,128)(2,1)}, bf16[256,128]{1,0:T(8,128)(2,1)}) custom-call(s32[1]{0:T(128)} %bitcast.q_ref, bf16[8,16,2048]{2,1,0:T(8,128)(2,1)} %copy-done.5, bf16[8,16,2048]{2,1,0:T(8,128)(2,1)} %collective-permute-done.7.refs_1_, bf16[256,256]{1,0:T(8,128)(2,1)} %constant.19.clone.refs_2_, ...), custom_call_target="tpu_custom_call", output_to_operand_aliasing={{0}: (4, {}), {1}: (5, {})} | custom-call | flops 134217728 | bytes 2097152 | tf_op jit(solution)/shard_map/rotate_cast/pallas_call | solution.py:225
  95.1 1.0 copy-done.4
  96.1 5.8 %rotate_cast.8 = (bf16[128,16384]{1,0:T(8,128)(2,1)}, bf16[128,128]{1,0:T(8,128)(2,1)}) custom-call(s32[1]{0:T(128)} %bitcast.q_ref, bf16[8,32,2048]{2,1,0:T(8,128)(2,1)} %copy-done.3, bf16[8,32,2048]{2,1,0:T(8,128)(2,1)} %copy-done.4, bf16[256,256]{1,0:T(8,128)(2,1)} %constant.19.clone.refs_2_, ...), custom_call_target="tpu_custom_call", output_to_operand_aliasing={{0}: (4, {}), {1}: (5, {})} | custom-call | flops 268435456 | bytes 4194304 | tf_op jit(solution)/shard_map/rotate_cast/pallas_call | solution.py:225
  (15 shorter events, 0.0 us)
Async XLA Ops:
  3.7 27.4 %all-to-all-start = ((bf16[8,48,2048]{2,1,0:T(8,128)(2,1)}), bf16[8,48,2048]{2,1,0:T(8,128)(2,1)S(1)}, u32[]{:S(2)}, u32[]{:S(2)}) async-start(bf16[8,48,2048]{2,1,0:T(8,128)(2,1)} %pick_rows.5), calls=%async_computation | async-start | bytes 3145728 | tf_op jit(solution)/shard_map/all_to_all | solution.py:281
  31.1 8.7 %copy-start = (bf16[8,48,2048]{2,1,0:T(8,128)(2,1)}, bf16[8,48,2048]{2,1,0:T(8,128)(2,1)S(1)}, u32[]{:S(2)}) copy-start(bf16[8,48,2048]{2,1,0:T(8,128)(2,1)S(1)} %all-to-all-done.refs_0_) | copy-start | bytes 4718596
  31.1 19.8 %collective-permute-start.5 = (bf16[8,48,2048]{2,1,0:T(8,128)(2,1)S(1)}, bf16[8,48,2048]{2,1,0:T(8,128)(2,1)}, u32[]{:S(2)}, u32[]{:S(2)}) collective-permute-start(bf16[8,48,2048]{2,1,0:T(8,128)(2,1)S(1)} %all-to-all-done.refs_0_), channel_id=1, source_target_pairs={{0,2},{1,7},{2,4},{3,1},{4,6},{5,3},{6,0},{7,5},{8,10},{9,15},{10,... | collective-permute-start | bytes 4718600 | tf_op jit(solution)/shard_map/ppermute | solution.py:278
  33.6 20.1 %collective-permute-start = (bf16[8,48,2048]{2,1,0:T(8,128)(2,1)S(1)}, bf16[8,48,2048]{2,1,0:T(8,128)(2,1)}, u32[]{:S(2)}, u32[]{:S(2)}) collective-permute-start(bf16[8,48,2048]{2,1,0:T(8,128)(2,1)S(1)} %all-to-all-done.refs_0_), channel_id=1, source_target_pairs={{0,1},{1,0},{2,3},{3,2},{4,5},{5,4},{6,7},{7,6},{8,9},{9,8},{10,11... | collective-permute-start | bytes 4718600 | tf_op jit(solution)/shard_map/ppermute | solution.py:275
  33.6 28.1 %all-to-all-start.1 = ((bf16[8,32,2048]{2,1,0:T(8,128)(2,1)}), bf16[8,32,2048]{2,1,0:T(8,128)(2,1)S(1)}, u32[]{:S(2)}, u32[]{:S(2)}) async-start(bf16[8,32,2048]{2,1,0:T(8,128)(2,1)} %pick_rows.4), calls=%async_computation.1 | async-start | bytes 2097152 | tf_op jit(solution)/shard_map/all_to_all | solution.py:281
  51.0 27.4 %collective-permute-start.6 = (bf16[8,48,2048]{2,1,0:T(8,128)(2,1)}, bf16[8,48,2048]{2,1,0:T(8,128)(2,1)}, u32[]{:S(2)}, u32[]{:S(2)}) collective-permute-start(bf16[8,48,2048]{2,1,0:T(8,128)(2,1)} %collective-permute-done.5.refs_0_), channel_id=1, source_target_pairs={{0,1},{1,0},{2,3},{3,2},{4,5},{5,4},{6,7},{7,6},{8,9},{9,8},{10,11... | collective-permute-start | bytes 4718600 | tf_op jit(solution)/shard_map/ppermute | solution.py:275
  61.7 4.9 %copy-start.1 = (bf16[8,32,2048]{2,1,0:T(8,128)(2,1)}, bf16[8,32,2048]{2,1,0:T(8,128)(2,1)S(1)}, u32[]{:S(2)}) copy-start(bf16[8,32,2048]{2,1,0:T(8,128)(2,1)S(1)} %all-to-all-done.1.refs_0_) | copy-start | bytes 3145732
  61.8 4.9 %collective-permute-start.3 = (bf16[8,32,2048]{2,1,0:T(8,128)(2,1)S(1)}, bf16[8,32,2048]{2,1,0:T(8,128)(2,1)}, u32[]{:S(2)}, u32[]{:S(2)}) collective-permute-start(bf16[8,32,2048]{2,1,0:T(8,128)(2,1)S(1)} %all-to-all-done.1.refs_0_), channel_id=1, source_target_pairs={{0,1},{1,0},{2,3},{3,2},{4,5},{5,4},{6,7},{7,6},{8,9},{9,8},{10,11... | collective-permute-start | bytes 3145736 | tf_op jit(solution)/shard_map/ppermute | solution.py:275
  61.8 14.2 %collective-permute-start.1 = (bf16[8,32,2048]{2,1,0:T(8,128)(2,1)S(1)}, bf16[8,32,2048]{2,1,0:T(8,128)(2,1)S(1)}, u32[]{:S(2)}, u32[]{:S(2)}) collective-permute-start(bf16[8,32,2048]{2,1,0:T(8,128)(2,1)S(1)} %all-to-all-done.1.refs_0_), channel_id=1, source_target_pairs={{0,2},{1,7},{2,4},{3,1},{4,6},{5,3},{6,0},{7,5},{8,10},{9,15},{10,... | collective-permute-start | bytes 3145736 | tf_op jit(solution)/shard_map/ppermute | solution.py:278
  63.2 12.9 %all-to-all-start.2 = ((bf16[8,16,2048]{2,1,0:T(8,128)(2,1)}), bf16[8,16,2048]{2,1,0:T(8,128)(2,1)S(1)}, u32[]{:S(2)}, u32[]{:S(2)}) async-start(bf16[8,16,2048]{2,1,0:T(8,128)(2,1)} %pick_rows.3), calls=%async_computation.2 | async-start | bytes 1048576 | tf_op jit(solution)/shard_map/all_to_all | solution.py:281
  76.1 10.3 %copy-start.2 = (bf16[8,16,2048]{2,1,0:T(8,128)(2,1)}, bf16[8,16,2048]{2,1,0:T(8,128)(2,1)S(1)}, u32[]{:S(2)}) copy-start(bf16[8,16,2048]{2,1,0:T(8,128)(2,1)S(1)} %all-to-all-done.2.refs_0_) | copy-start | bytes 1572868
  76.1 10.3 %collective-permute-start.4 = (bf16[8,16,2048]{2,1,0:T(8,128)(2,1)S(1)}, bf16[8,16,2048]{2,1,0:T(8,128)(2,1)S(1)}, u32[]{:S(2)}, u32[]{:S(2)}) collective-permute-start(bf16[8,16,2048]{2,1,0:T(8,128)(2,1)S(1)} %all-to-all-done.2.refs_0_), channel_id=1, source_target_pairs={{0,2},{1,7},{2,4},{3,1},{4,6},{5,3},{6,0},{7,5},{8,10},{9,15},{10,... | collective-permute-start | bytes 1572872 | tf_op jit(solution)/shard_map/ppermute | solution.py:278
  76.1 10.3 %copy-start.3 = (bf16[8,32,2048]{2,1,0:T(8,128)(2,1)}, bf16[8,32,2048]{2,1,0:T(8,128)(2,1)S(1)}, u32[]{:S(2)}) copy-start(bf16[8,32,2048]{2,1,0:T(8,128)(2,1)S(1)} %collective-permute-done.1.refs_0_) | copy-start | bytes 3145732
  76.1 19.0 %collective-permute-start.2 = (bf16[8,32,2048]{2,1,0:T(8,128)(2,1)S(1)}, bf16[8,32,2048]{2,1,0:T(8,128)(2,1)S(1)}, u32[]{:S(2)}, u32[]{:S(2)}) collective-permute-start(bf16[8,32,2048]{2,1,0:T(8,128)(2,1)S(1)} %collective-permute-done.1.refs_0_), channel_id=1, source_target_pairs={{0,1},{1,0},{2,3},{3,2},{4,5},{5,4},{6,7},{7,6},{8,9},{9,8},{10,11... | collective-permute-start | bytes 3145736 | tf_op jit(solution)/shard_map/ppermute | solution.py:275
  78.4 8.8 %collective-permute-start.8 = (bf16[8,16,2048]{2,1,0:T(8,128)(2,1)S(1)}, bf16[8,16,2048]{2,1,0:T(8,128)(2,1)S(1)}, u32[]{:S(2)}, u32[]{:S(2)}) collective-permute-start(bf16[8,16,2048]{2,1,0:T(8,128)(2,1)S(1)} %all-to-all-done.2.refs_0_), channel_id=1, source_target_pairs={{0,1},{1,0},{2,3},{3,2},{4,5},{5,4},{6,7},{7,6},{8,9},{9,8},{10,11... | collective-permute-start | bytes 1572872 | tf_op jit(solution)/shard_map/ppermute | solution.py:275
  86.4 5.1 %copy-start.5 = (bf16[8,16,2048]{2,1,0:T(8,128)(2,1)}, bf16[8,16,2048]{2,1,0:T(8,128)(2,1)S(1)}, u32[]{:S(2)}) copy-start(bf16[8,16,2048]{2,1,0:T(8,128)(2,1)S(1)} %collective-permute-done.4.refs_0_) | copy-start | bytes 1572868
  86.4 5.1 %collective-permute-start.7 = (bf16[8,16,2048]{2,1,0:T(8,128)(2,1)S(1)}, bf16[8,16,2048]{2,1,0:T(8,128)(2,1)}, u32[]{:S(2)}, u32[]{:S(2)}) collective-permute-start(bf16[8,16,2048]{2,1,0:T(8,128)(2,1)S(1)} %collective-permute-done.4.refs_0_), channel_id=1, source_target_pairs={{0,1},{1,0},{2,3},{3,2},{4,5},{5,4},{6,7},{7,6},{8,9},{9,8},{10,11... | collective-permute-start | bytes 1572872 | tf_op jit(solution)/shard_map/ppermute | solution.py:275
  87.1 0.8 copy-start.6
  95.1 1.0 copy-start.4

commit v3 on v2

v3 whole, which is shorter than its diff:
```python
import functools
import itertools
import math

import jax
import jax.numpy as jnp
import numpy as np
from jax import lax
from jax.experimental import pallas as pl
from jax.experimental.pallas import tpu as pltpu
from jax.sharding import PartitionSpec as P

SIDE = 128
UNIT = 16
LOCAL = 2048
BLOCKS = LOCAL // SIDE
SHARDS = 8
PARTS = ((0, 0, 0, 8), (0, 2, 8, 8), (2, 6, 16, 0))
FLIPPED = (0, 0, 0)
FETCH = (
    ((0, 1, 0), (0, 3, 0)),
    ((1, 3, 0), (1, 1, 1)),
    ((0, 2, 0), (1, 2, 1)),
    ((1, 0, 0), None),
)
VMEM = 60 * 2**20


def signs(order):
    h = np.ones((1, 1), np.float32)
    while h.shape[0] < order:
        h = np.block([[h, h], [h, -h]])
    return h


def two_blocks():
    h = signs(SIDE)
    z = np.zeros_like(h)
    return jnp.asarray(np.block([[h, z], [z, h]]) / SIDE, jnp.bfloat16)


def butterflies(values):
    span = 1
    values = list(values)
    while span < len(values):
        for i in range(len(values)):
            if i & span == 0:
                lo, hi = values[i], values[i + span]
                values[i], values[i + span] = lo + hi, lo - hi
        span *= 2
    return values


def by_role(role, values):
    result = jnp.int32(values[3])
    for r in range(3):
        result = jnp.where(role == r, values[r], result)
    return result


def shard_at(here, role, slot, back):
    steps = [FETCH[r][slot] or (0, 0, 0) for r in range(4)]
    dy = by_role(role, [s[0] for s in steps])
    dz = by_role(role, [(4 - s[1]) % 4 if back else s[1] for s in steps])
    return ((here // 4) ^ dy) * 4 + ((here + dz) & 3)


def pick_kernel(part, share, ranks, f_ref, r_ref, out_hbm, down_hbm, *refs):
    o0, no, d0, nd = part
    n = no + nd
    sends, (pairs, stage, sems, gone) = refs[:3], refs[3:]
    here, role = f_ref[0], r_ref[0]
    to = [shard_at(here, role, slot, True) for slot in range(2)] + [here]
    copies = []
    for i in range(3):
        rank = ranks[to[i]]
        mine = []
        for u in range(no):
            for h in range(2):
                block = share[2 * (o0 + u) + h]
                row = rank * 64 + lax.rem(block, 8) // 2 * 16
                mine.append(
                    pltpu.make_async_copy(
                        out_hbm.at[block // 8, pl.ds(pl.multiple_of(row, 16), 16), :],
                        pairs.at[i, u, h],
                        sems.at[i, len(mine)],
                    )
                )
        for u in range(nd):
            block = share[d0 + u]
            row = rank * 128 + lax.rem(block, 8) * 16
            mine.append(
                pltpu.make_async_copy(
                    down_hbm.at[block // 8, pl.ds(pl.multiple_of(row, 16), 16), :],
                    stage.at[i, u],
                    sems.at[i, len(mine)],
                )
            )
        for c in mine:
            c.start()
        copies.append(mine)
    leaving = []
    for i in range(3):
        for c in copies[i]:
            c.wait()
        for u in range(no):
            halves = []
            for h in range(2):
                odd = lax.rem(share[2 * (o0 + u) + h], 2) == 1
                rows = pairs[i, u, h].astype(jnp.float32)
                halves.append(jnp.where(odd, rows[8:], rows[:8]))
            stage[i, nd + u] = jnp.concatenate(halves, 0).astype(jnp.bfloat16)
        c = pltpu.make_async_copy(stage.at[i], sends[i], gone.at[i])
        c.start()
        leaving.append(c)
    for c in leaving:
        c.wait()


def pick(part, share, ranks, here, role, out_weight, down_weight):
    o0, no, d0, nd = part
    n = no + nd
    shape = (n, UNIT, LOCAL)
    return pl.pallas_call(
        functools.partial(pick_kernel, part),
        grid_spec=pltpu.PrefetchScalarGridSpec(
            num_scalar_prefetch=4,
            grid=(),
            in_specs=[pl.BlockSpec(memory_space=pltpu.HBM)] * 2,
            out_specs=[pl.BlockSpec(memory_space=pltpu.HBM)] * 3,
            scratch_shapes=[
                pltpu.VMEM((3, max(no, 1), 2, UNIT, LOCAL), jnp.bfloat16),
                pltpu.VMEM((3,) + shape, jnp.bfloat16),
                pltpu.SemaphoreType.DMA((3, 2 * no + nd)),
                pltpu.SemaphoreType.DMA((3,)),
            ],
        ),
        out_shape=[jax.ShapeDtypeStruct(shape, jnp.bfloat16)] * 3,
        compiler_params=pltpu.CompilerParams(vmem_limit_bytes=VMEM),
        cost_estimate=pl.CostEstimate(
            flops=0, bytes_accessed=9 * math.prod(shape) * 2, transcendentals=0
        ),
        name="pick_rows",
    )(share, ranks, here, role, out_weight, down_weight)


def spread(shards_in, rot, work):
    for at, x in shards_in:
        stack = jnp.concatenate(
            [x[:, c * 256 : (c + 1) * 256] for c in range(BLOCKS // 2)], 0
        )
        y = jnp.dot(stack, rot, preferred_element_type=jnp.float32)
        parts = butterflies(
            y[c * UNIT : (c + 1) * UNIT, h * SIDE : (h + 1) * SIDE]
            for c in range(BLOCKS // 2)
            for h in range(2)
        )
        for k in range(BLOCKS):
            work[at * BLOCKS + k] = parts[k]


def finish(quant, scales, work):
    lane = lax.broadcasted_iota(jnp.int32, (UNIT, SIDE), 1)
    top = jnp.zeros((UNIT, SIDE), jnp.float32)
    for k in range(BLOCKS):
        parts = butterflies(work[f * BLOCKS + k] for f in range(SHARDS))
        for f in range(SHARDS):
            a = f * BLOCKS + k
            m = jnp.max(jnp.abs(parts[f]), axis=1, keepdims=True)
            s = (m + 1e-06).astype(jnp.bfloat16).astype(jnp.float32)
            quant[:, a * SIDE : (a + 1) * SIDE] = (parts[f] * (1.0 / s)).astype(
                jnp.bfloat16
            )
            top = jnp.where(lane == a, m, top)
    scales[...] = (top + 1e-06).astype(jnp.bfloat16)


def rotate_kernel(part, n_alias, f_ref, r_ref, *refs):
    o0, no, d0, nd = part
    n = no + nd
    messages, local, rot_ref = refs[:4], refs[4], refs[5]
    outs = list(refs[6 + n_alias : -6])
    quants, tops, even, odd, left, left_top = refs[-6:]
    kinds = []
    if nd:
        kinds.append((0, nd, d0, outs.pop(0), outs.pop(0)))
    if no:
        kinds.append((nd, no, o0, outs.pop(0), outs.pop(0)))
    here, role = f_ref[0], r_ref[0]

    rot = rot_ref[...]
    places = []
    for m in range(8):
        of, slot = role ^ (m // 2), m % 2
        gap = (of == 3) & (slot == 1)
        at = shard_at(here, of, slot, False)
        places.append((m // 2, slot, gap, jnp.where(gap, here, at) if slot else at))

    def take(t, work):
        shards_in = []
        for m, slot, gap, at in places:
            x = messages[m][slot * n + t]
            if slot:
                x = jnp.where(gap, local[t], x)
            shards_in.append((at, x))
        spread(shards_in, rot, work)

    def leave(t, begin):
        for first, count, row, quant, scales in kinds:

            @pl.when((t >= first) & (t < first + count))
            def _():
                rows = pl.ds(pl.multiple_of((row + t - first) * UNIT, UNIT), UNIT)
                for c in (
                    pltpu.make_async_copy(quants.at[t], quant.at[rows, :], left.at[t]),
                    pltpu.make_async_copy(
                        tops.at[t], scales.at[rows, :], left_top.at[t]
                    ),
                ):
                    c.start() if begin else c.wait()

    def give(t, work):
        finish(quants.at[t], tops.at[t], work)

    take(0, even)

    def pair(j, _):
        t = 2 * j
        take(t + 1, odd)
        give(t, even)
        leave(t, True)

        @pl.when(t + 2 < n)
        def _():
            take(t + 2, even)
            give(t + 1, odd)

        @pl.when(t + 2 >= n)
        def _():
            give(t + 1, odd)

        leave(t + 1, True)
        return 0

    lax.fori_loop(0, n // 2, pair, 0)

    def settle(t, _):
        leave(t, False)
        return 0

    lax.fori_loop(0, n, settle, 0)


def rotate(part, messages, local, here, role, rot, before):
    o0, no, d0, nd = part
    n = no + nd
    columns = SHARDS * LOCAL
    shapes = [(128, columns), (128, SIDE), (256, columns), (256, SIDE)]
    used = [i for i in (2, 3, 0, 1) if (no, no, nd, nd)[i]]
    operands = list(messages) + [local, rot]
    aliases = {}
    for i, t in enumerate(used):
        if before[t] is not None:
            aliases[2 + len(operands)] = i
            operands.append(before[t])
    hbm = pl.BlockSpec(memory_space=pltpu.HBM)
    in_specs = [hbm] * len(operands)
    in_specs[:6] = [pl.BlockSpec(memory_space=pltpu.VMEM)] * 6
    elements = n * UNIT * columns
    work = pltpu.VMEM((SHARDS * BLOCKS, UNIT, SIDE), jnp.float32)
    results = pl.pallas_call(
        functools.partial(rotate_kernel, part, len(aliases)),
        grid_spec=pltpu.PrefetchScalarGridSpec(
            num_scalar_prefetch=2,
            grid=(),
            in_specs=in_specs,
            out_specs=[hbm] * len(used),
            scratch_shapes=[
                pltpu.VMEM((n, UNIT, columns), jnp.bfloat16),
                pltpu.VMEM((n, UNIT, SIDE), jnp.bfloat16),
                work,
                work,
                pltpu.SemaphoreType.DMA((n,)),
                pltpu.SemaphoreType.DMA((n,)),
            ],
        ),
        out_shape=[jax.ShapeDtypeStruct(shapes[t], jnp.bfloat16) for t in used],
        input_output_aliases=aliases,
        compiler_params=pltpu.CompilerParams(vmem_limit_bytes=24 * 2**20),
        cost_estimate=pl.CostEstimate(
            flops=elements * 256, bytes_accessed=elements * 4, transcendentals=0
        ),
        name="rotate_cast",
    )(here, role, *operands)
    after = list(before)
    for t, r in zip(used, results):
        after[t] = r
    return after


def pairs_of(target):
    def index(yl, z, yh, x, c):
        return (yl * 4 + z) * 16 + (yh * 4 + x) * 2 + c

    return [
        (index(*d), index(*target(*d)))
        for d in itertools.product(range(2), range(4), range(2), range(4), range(2))
    ]


def fetch_pairs(slot, flipped):
    def target(yl, z, yh, x, c):
        dy, dz, dh = FETCH[(x % 2 ^ flipped) * 2 + c][slot] or (0, 0, 0)
        return yl ^ dy, (z - dz) % 4, yh ^ dh, x, c

    return pairs_of(target)


OTHER = pairs_of(lambda yl, z, yh, x, c: (yl, z, yh, x, 1 - c))
ALONG = pairs_of(lambda yl, z, yh, x, c: (yl, z, yh, (x + 1 + 2 * c) % 4, c))
AXES = ("fsdp", "replica")


def shards(out_weight, down_weight, layer_share, rank_map):
    here = lax.axis_index("fsdp").astype(jnp.int32)[None]
    seat = (lax.axis_index("replica") % 4).astype(jnp.int32)[None]
    roles = [seat ^ 2 * f for f in FLIPPED]
    rot = two_blocks()
    picked = [
        pick(part, layer_share, rank_map, here, role, out_weight, down_weight)
        for part, role in zip(PARTS, roles)
    ]

    def fetch(k, sends):
        return [
            lax.ppermute(m, AXES, fetch_pairs(s, FLIPPED[k]))
            for s, m in enumerate(sends)
        ]

    def onward(message):
        return lax.ppermute(message, AXES, ALONG)

    def swap(message):
        return lax.ppermute(message, AXES, OTHER)

    def turn(k, messages, done):
        return rotate(PARTS[k], messages, picked[k][2], here, roles[k], rot, done)

    def tied(value, *others):
        return lax.optimization_barrier((value, *others))[0]

    done = [None] * 4
    own0 = fetch(0, picked[0][:2])
    own1 = fetch(1, picked[1][:2])
    own0 = jnp.concatenate(own0)
    own0 = tied(own0, *picked[2])
    along0 = onward(own0)
    other0 = swap(own0)
    own2 = fetch(2, [tied(m, own0) for m in picked[2][:2]])
    own1 = jnp.concatenate(own1)
    along1 = onward(own1)
    other1 = swap(own1)
    along_other0 = swap(tied(along0, own1))
    done = turn(0, [own0, other0, along0, along_other0], done)
    along_other1 = swap(tied(along1, done[2]))
    own2 = jnp.concatenate([tied(m, done[2]) for m in own2])
    along2 = onward(own2)
    other2 = swap(own2)
    done = turn(1, [own1, other1, along1, along_other1], done)
    along_other2 = swap(tied(along2, done[2]))
    done = turn(2, [own2, other2, along2, along_other2], done)
    return tuple(d[None] for d in done)


def solution(mesh):
    return jax.shard_map(
        shards,
        mesh=mesh,
        in_specs=(P(None, None, "fsdp"), P(None, None, "fsdp"), P(), P()),
        out_specs=(P("fsdp", None, None),) * 4,
        check_vma=False,
    )
```

time: 103 us -> 81.2 us (0.79)
  waiting for transfers between devices: 31.8 us -> 8.75 us
  starting transfers between devices: 23.7 us -> 41.5 us
  Pallas kernels: 43.8 us -> 29.2 us
  local copies, waits for them, and re-layouts: 1.83 us -> 0.17 us
    ppermute x9 -> x15, starting transfers between devices: 9.61 us -> 41.5 us  [the longest x6 21.8 us: swap(): return lax.ppermute(message, AXES, OTHER)]
    all_to_all x3 -> x0, waiting for transfers between devices: 20.7 us -> none  [to_owner(): return lax.all_to_all(send, 'fsdp', split_axis=0, concat_axis=0, tiled=True)]
    pallas_call x6 -> x3, Pallas kernels: 34.8 us -> 18.7 us  [rotate(): pl.pallas_call(functools.partial(rotate_kernel, part, len(aliases)), grid...]
    all_to_all x3 -> x0, starting transfers between devices: 14.1 us -> none  [to_owner(): return lax.all_to_all(send, 'fsdp', split_axis=0, concat_axis=0, tiled=True)]
    ppermute x9 -> x15, waiting for transfers between devices: 11.1 us -> 8.75 us  [the longest x6 5.63 us: fetch(): lax.ppermute(m, AXES, fetch_pairs(s, FLIPPED[k]))]
    unnamed x14, local copies, waits for them, and re-layouts: 1.83 us -> 0.1 us
    pallas_call x3, Pallas kernels: 9.02 us -> 10.5 us  [pick(): pl.pallas_call(functools.partial(pick_kernel, part), grid_spec=pltpu.Pref...]
  transfers between devices with their start and end apart: 12 -> 15, of which waited for: 3 -> 5; matrix products, arithmetic and copies ran while one was open for 0% -> 0% of each run, Pallas kernels for 34% -> 26%
where the time goes in v3:
time: 81.2 us; the launch traced here: 80.6 us
  starting transfers between devices  41.5 us (51%)
  Pallas kernels  29.2 us (36%)
  waiting for transfers between devices  8.75 us (11%)
  between operations  0.91 us (1%)
    ppermute x6, starting transfers between devices, swap(): return lax.ppermute(message, AXES, OTHER)  21.8 us
    ppermute x6, starting transfers between devices, fetch(): lax.ppermute(m, AXES, fetch_pairs(s, FLIPPED[k]))  19.5 us
    pallas_call x3, Pallas kernels, rotate(): pl.pallas_call(functools.partial(rotate_kernel, part, len(aliases)), grid...  18.7 us
    pallas_call x3, Pallas kernels, pick(): pl.pallas_call(functools.partial(pick_kernel, part), grid_spec=pltpu.Pref...  10.5 us
    ppermute x6, waiting for transfers between devices, fetch(): lax.ppermute(m, AXES, fetch_pairs(s, FLIPPED[k]))  5.63 us
    ppermute x6, waiting for transfers between devices, swap(): return lax.ppermute(message, AXES, OTHER)  1.92 us
  transfers between devices with their start and end apart: 15, of which 5 were waited for; matrix products, arithmetic and copies ran while one was open for 0% of the time, Pallas kernels for 26%

profile of v3, /device:TPU:1, one launch (start us, length us, event | category | flops | bytes accessed | tf_op | source)
XLA Modules:
  0.0 80.6 jit_solution(13172647249923098986)
XLA Ops:
  0.6 3.2 %pick_rows.4 = (bf16[8,16,2048]{2,1,0:T(8,128)(2,1)}, bf16[8,16,2048]{2,1,0:T(8,128)(2,1)}, bf16[8,16,2048]{2,1,0:T(8,128)(2,1)}) custom-call(s32[16]{0:T(128)} %share.5, s32[8]{0:T(128)} %ranks.5, s32[1]{0:T(128)} %bitcast.f_ref, s32[1]{0:T(128)} %bitcast.1.r_ref, bf16[2,512,2048]{2,1,0:T(8,128)(2,1)} %out_hbm.5, bf16[2,1024,2048]{2,1,0:T(8,128)(2,1)} %down_hbm.5), custom_call_target="tpu_custom_call" | custom-call | bytes 4718592 | tf_op jit(solution)/shard_map/pick_rows/pallas_call | solution.py:124
  3.8 3.5 %collective-permute-start = (bf16[8,16,2048]{2,1,0:T(8,128)(2,1)}, bf16[8,16,2048]{2,1,0:T(8,128)(2,1)S(1)}, u32[]{:S(2)}, u32[]{:S(2)}) collective-permute-start(bf16[8,16,2048]{2,1,0:T(8,128)(2,1)} %get-tuple-element.30), channel_id=1, source_target_pairs={{0,48},{1,81},{2,34},{3,67},{4,52},{5,85},{6,38},{7,71},{8,56},{9,... | collective-permute-start | bytes 1572872 | tf_op jit(solution)/shard_map/ppermute | solution.py:336
  7.4 5.5 %collective-permute-start.1 = (bf16[8,16,2048]{2,1,0:T(8,128)(2,1)}, bf16[8,16,2048]{2,1,0:T(8,128)(2,1)S(1)}, u32[]{:S(2)}, u32[]{:S(2)}) collective-permute-start(bf16[8,16,2048]{2,1,0:T(8,128)(2,1)} %get-tuple-element.31), channel_id=1, source_target_pairs={{0,16},{1,121},{2,106},{3,3},{4,20},{5,125},{6,110},{7,7},{8,24},{... | collective-permute-start | bytes 1572872 | tf_op jit(solution)/shard_map/ppermute | solution.py:336
  12.9 3.6 %pick_rows.5 = (bf16[10,16,2048]{2,1,0:T(8,128)(2,1)}, bf16[10,16,2048]{2,1,0:T(8,128)(2,1)}, bf16[10,16,2048]{2,1,0:T(8,128)(2,1)}) custom-call(s32[16]{0:T(128)} %share.5, s32[8]{0:T(128)} %ranks.5, s32[1]{0:T(128)} %bitcast.f_ref, s32[1]{0:T(128)} %bitcast.1.r_ref, bf16[2,512,2048]{2,1,0:T(8,128)(2,1)} %out_hbm.5, bf16[2,1024,2048]{2,1,0:T(8,128)(2,1)} %down_hbm.5), custom_call_target="tpu_custom_call" | custom-call | bytes 5898240 | tf_op jit(solution)/shard_map/pick_rows/pallas_call | solution.py:124
  16.5 0.1 collective-permute-start.5
  16.6 4.6 %collective-permute-start.6 = (bf16[10,16,2048]{2,1,0:T(8,128)(2,1)}, bf16[10,16,2048]{2,1,0:T(8,128)(2,1)S(1)}, u32[]{:S(2)}, u32[]{:S(2)}) collective-permute-start(bf16[10,16,2048]{2,1,0:T(8,128)(2,1)} %get-tuple-element.37), channel_id=1, source_target_pairs={{0,16},{1,121},{2,106},{3,3},{4,20},{5,125},{6,110},{7,7},{8,24},{... | collective-permute-start | bytes 1966088 | tf_op jit(solution)/shard_map/ppermute | solution.py:336
  21.2 3.7 %pick_rows.3 = (bf16[6,16,2048]{2,1,0:T(8,128)(2,1)}, bf16[6,16,2048]{2,1,0:T(8,128)(2,1)}, bf16[6,16,2048]{2,1,0:T(8,128)(2,1)}) custom-call(s32[16]{0:T(128)} %share.5, s32[8]{0:T(128)} %ranks.5, s32[1]{0:T(128)} %bitcast.f_ref, s32[1]{0:T(128)} %bitcast.1.r_ref, bf16[2,512,2048]{2,1,0:T(8,128)(2,1)} %out_hbm.5, bf16[2,1024,2048]{2,1,0:T(8,128)(2,1)} %down_hbm.5), custom_call_target="tpu_custom_call" | custom-call | bytes 3538944 | tf_op jit(solution)/shard_map/pick_rows/pallas_call | solution.py:124
  24.9 0.0 collective-permute-done
  24.9 0.1 pad_maximum_fusion.refs_0_
  25.0 0.0 copy-start
  25.0 0.1 collective-permute-start.4
  25.1 3.3 %collective-permute-done.5 = bf16[10,16,2048]{2,1,0:T(8,128)(2,1)S(1)} collective-permute-done((bf16[10,16,2048]{2,1,0:T(8,128)(2,1)}, bf16[10,16,2048]{2,1,0:T(8,128)(2,1)S(1)}, u32[]{:S(2)}, u32[]{:S(2)}) %collective-permute-start.5) | collective-permute-done | bytes 655392 | tf_op jit(solution)/shard_map/ppermute | solution.py:336
  28.5 1.9 %collective-permute-done.6 = bf16[10,16,2048]{2,1,0:T(8,128)(2,1)S(1)} collective-permute-done((bf16[10,16,2048]{2,1,0:T(8,128)(2,1)}, bf16[10,16,2048]{2,1,0:T(8,128)(2,1)S(1)}, u32[]{:S(2)}, u32[]{:S(2)}) %collective-permute-start.6) | collective-permute-done | bytes 655392 | tf_op jit(solution)/shard_map/ppermute | solution.py:336
  30.4 0.1 collective-permute-start.12
  30.5 9.4 %collective-permute-start.3 = (bf16[16,16,2048]{2,1,0:T(8,128)(2,1)S(1)}, bf16[16,16,2048]{2,1,0:T(8,128)(2,1)S(1)}, u32[]{:S(2)}, u32[]{:S(2)}) collective-permute-start(bf16[16,16,2048]{2,1,0:T(8,128)(2,1)S(1)} %pad_maximum_fusion.refs_0_), channel_id=1, source_target_pairs={{0,1},{1,0},{2,3},{3,2},{4,5},{5,4},{6,7},{7,6},{8,9},{9,8},{10,11... | collective-permute-start | bytes 3145736 | tf_op jit(solution)/shard_map/ppermute | solution.py:344
  39.9 0.0 collective-permute-done.4.refs_2_
  39.9 5.9 %collective-permute-start.7 = (bf16[16,16,2048]{2,1,0:T(8,128)(2,1)S(1)}, bf16[16,16,2048]{2,1,0:T(8,128)(2,1)S(1)}, u32[]{:S(2)}, u32[]{:S(2)}) collective-permute-start(bf16[16,16,2048]{2,1,0:T(8,128)(2,1)S(1)} %collective-permute-done.4.refs_2_), channel_id=1, source_target_pairs={{0,1},{1,0},{2,3},{3,2},{4,5},{5,4},{6,7},{7,6},{8,9},{9,8},{10,11... | collective-permute-start | bytes 3145736 | tf_op jit(solution)/shard_map/ppermute | solution.py:344
  45.8 5.7 %collective-permute-start.8 = (bf16[6,16,2048]{2,1,0:T(8,128)(2,1)S(1)}, bf16[6,16,2048]{2,1,0:T(8,128)(2,1)S(1)}, u32[]{:S(2)}, u32[]{:S(2)}) collective-permute-start(bf16[6,16,2048]{2,1,0:T(8,128)(2,1)S(1)} %copy-done.5), channel_id=1, source_target_pairs={{0,16},{1,121},{2,106},{3,3},{4,20},{5,125},{6,110},{7,7},{8,24},{... | collective-permute-start | bytes 1179656 | tf_op jit(solution)/shard_map/ppermute | solution.py:336
  51.6 0.1 collective-permute-start.2
  51.6 0.0 collective-permute-done.3.refs_1_
  51.6 0.1 collective-permute-start.11
  51.7 0.0 collective-permute-done.7.refs_3_
  51.8 6.2 %rotate_cast.3 = (bf16[256,16384]{1,0:T(8,128)(2,1)}, bf16[256,128]{1,0:T(8,128)(2,1)}) custom-call(s32[1]{0:T(128)} %bitcast.f_ref, s32[1]{0:T(128)} %bitcast.1.r_ref, bf16[16,16,2048]{2,1,0:T(8,128)(2,1)S(1)} %pad_maximum_fusion.refs_0_, bf16[16,16,2048]{2,1,0:T(8,128)(2,1)S(1)} %collective-permute-done.3.refs_1_, ...), custom_call_target="tpu_custom_call" | custom-call | flops 536870912 | bytes 8388608 | tf_op jit(solution)/shard_map/rotate_cast/pallas_call | solution.py:271
  58.0 1.9 %collective-permute-start.13 = (bf16[20,16,2048]{2,1,0:T(8,128)(2,1)S(1)}, bf16[20,16,2048]{2,1,0:T(8,128)(2,1)S(1)}, u32[]{:S(2)}, u32[]{:S(2)}) collective-permute-start(bf16[20,16,2048]{2,1,0:T(8,128)(2,1)S(1)} %collective-permute-done.12.refs_2_), channel_id=1, source_target_pairs={{0,1},{1,0},{2,3},{3,2},{4,5},{5,4},{6,7},{7,6},{8,9},{9,8},{10,11... | collective-permute-start | bytes 3932168 | tf_op jit(solution)/shard_map/ppermute | solution.py:344
  59.9 0.5 collective-permute-done.2
  60.4 0.1 collective-permute-start.10
  60.5 2.2 %collective-permute-start.9 = (bf16[12,16,2048]{2,1,0:T(8,128)(2,1)S(1)}, bf16[12,16,2048]{2,1,0:T(8,128)(2,1)S(1)}, u32[]{:S(2)}, u32[]{:S(2)}) collective-permute-start(bf16[12,16,2048]{2,1,0:T(8,128)(2,1)S(1)} %constant_dynamic-update-slice_fusion.2.refs_0_), channel_id=1, source_target_pairs={{0,1},{1,0},{2,3},{3,2},{4,5},{5,4},{6,7},{7,6},{8,9},{9,8},{10,11... | collective-permute-start | bytes 2359304 | tf_op jit(solution)/shard_map/ppermute | solution.py:344
  62.8 7.6 %rotate_cast.4 = (bf16[256,16384]{1,0:T(8,128)(2,1)}, bf16[256,128]{1,0:T(8,128)(2,1)}, bf16[128,16384]{1,0:T(8,128)(2,1)}, bf16[128,128]{1,0:T(8,128)(2,1)}) custom-call(s32[1]{0:T(128)} %bitcast.f_ref, s32[1]{0:T(128)} %bitcast.1.r_ref, ...), custom_call_target="tpu_custom_call", output_to_operand_aliasing={{0}: (8, {}), {1}: (9, {})} | custom-call | flops 671088640 | bytes 10485760 | tf_op jit(solution)/shard_map/rotate_cast/pallas_call | solution.py:271
  70.4 1.2 %collective-permute-done.10.refs_2_ = bf16[12,16,2048]{2,1,0:T(8,128)(2,1)S(1)} collective-permute-done((bf16[12,16,2048]{2,1,0:T(8,128)(2,1)S(1)}, bf16[12,16,2048]{2,1,0:T(8,128)(2,1)S(1)}, u32[]{:S(2)}, u32[]{:S(2)}) %collective-permute-start.10) | collective-permute-done | bytes 786464 | tf_op jit(solution)/shard_map/ppermute | solution.py:341
  71.6 2.2 %collective-permute-start.14 = (bf16[12,16,2048]{2,1,0:T(8,128)(2,1)S(1)}, bf16[12,16,2048]{2,1,0:T(8,128)(2,1)S(1)}, u32[]{:S(2)}, u32[]{:S(2)}) collective-permute-start(bf16[12,16,2048]{2,1,0:T(8,128)(2,1)S(1)} %collective-permute-done.10.refs_2_), channel_id=1, source_target_pairs={{0,1},{1,0},{2,3},{3,2},{4,5},{5,4},{6,7},{7,6},{8,9},{9,8},{10,11... | collective-permute-start | bytes 2359304 | tf_op jit(solution)/shard_map/ppermute | solution.py:344
  73.8 1.9 %collective-permute-done.14.refs_3_ = bf16[12,16,2048]{2,1,0:T(8,128)(2,1)S(1)} collective-permute-done((bf16[12,16,2048]{2,1,0:T(8,128)(2,1)S(1)}, bf16[12,16,2048]{2,1,0:T(8,128)(2,1)S(1)}, u32[]{:S(2)}, u32[]{:S(2)}) %collective-permute-start.14) | collective-permute-done | bytes 786464 | tf_op jit(solution)/shard_map/ppermute | solution.py:344
  75.8 4.9 %rotate_cast.5 = (bf16[128,16384]{1,0:T(8,128)(2,1)}, bf16[128,128]{1,0:T(8,128)(2,1)}) custom-call(s32[1]{0:T(128)} %bitcast.f_ref, s32[1]{0:T(128)} %bitcast.1.r_ref, bf16[12,16,2048]{2,1,0:T(8,128)(2,1)S(1)} %constant_dynamic-update-slice_fusion.2.refs_0_, ...), custom_call_target="tpu_custom_call", output_to_operand_aliasing={{0}: (8, {}), {1}: (9, {})} | custom-call | flops 402653184 | bytes 6291456 | tf_op jit(solution)/shard_map/rotate_cast/pallas_call | solution.py:271
  (21 shorter events, 0.2 us)
Async XLA Ops:
  3.8 21.0 %collective-permute-start = (bf16[8,16,2048]{2,1,0:T(8,128)(2,1)}, bf16[8,16,2048]{2,1,0:T(8,128)(2,1)S(1)}, u32[]{:S(2)}, u32[]{:S(2)}) collective-permute-start(bf16[8,16,2048]{2,1,0:T(8,128)(2,1)} %get-tuple-element.30), channel_id=1, source_target_pairs={{0,48},{1,81},{2,34},{3,67},{4,52},{5,85},{6,38},{7,71},{8,56},{9,... | collective-permute-start | bytes 1572872 | tf_op jit(solution)/shard_map/ppermute | solution.py:336
  7.4 17.5 %collective-permute-start.1 = (bf16[8,16,2048]{2,1,0:T(8,128)(2,1)}, bf16[8,16,2048]{2,1,0:T(8,128)(2,1)S(1)}, u32[]{:S(2)}, u32[]{:S(2)}) collective-permute-start(bf16[8,16,2048]{2,1,0:T(8,128)(2,1)} %get-tuple-element.31), channel_id=1, source_target_pairs={{0,16},{1,121},{2,106},{3,3},{4,20},{5,125},{6,110},{7,7},{8,24},{... | collective-permute-start | bytes 1572872 | tf_op jit(solution)/shard_map/ppermute | solution.py:336
  16.5 11.9 %collective-permute-start.5 = (bf16[10,16,2048]{2,1,0:T(8,128)(2,1)}, bf16[10,16,2048]{2,1,0:T(8,128)(2,1)S(1)}, u32[]{:S(2)}, u32[]{:S(2)}) collective-permute-start(bf16[10,16,2048]{2,1,0:T(8,128)(2,1)} %get-tuple-element.36), channel_id=1, source_target_pairs={{0,48},{1,81},{2,34},{3,67},{4,52},{5,85},{6,38},{7,71},{8,56},{9,... | collective-permute-start | bytes 1966088 | tf_op jit(solution)/shard_map/ppermute | solution.py:336
  16.6 13.8 %collective-permute-start.6 = (bf16[10,16,2048]{2,1,0:T(8,128)(2,1)}, bf16[10,16,2048]{2,1,0:T(8,128)(2,1)S(1)}, u32[]{:S(2)}, u32[]{:S(2)}) collective-permute-start(bf16[10,16,2048]{2,1,0:T(8,128)(2,1)} %get-tuple-element.37), channel_id=1, source_target_pairs={{0,16},{1,121},{2,106},{3,3},{4,20},{5,125},{6,110},{7,7},{8,24},{... | collective-permute-start | bytes 1966088 | tf_op jit(solution)/shard_map/ppermute | solution.py:336
  25.0 20.8 %copy-start.5 = (bf16[6,16,2048]{2,1,0:T(8,128)(2,1)S(1)}, bf16[6,16,2048]{2,1,0:T(8,128)(2,1)}, u32[]{:S(2)}) copy-start(bf16[6,16,2048]{2,1,0:T(8,128)(2,1)} %get-tuple-element.42) | copy-start | bytes 1179652
  25.0 26.5 %copy-start.4 = (bf16[6,16,2048]{2,1,0:T(8,128)(2,1)S(1)}, bf16[6,16,2048]{2,1,0:T(8,128)(2,1)}, u32[]{:S(2)}) copy-start(bf16[6,16,2048]{2,1,0:T(8,128)(2,1)} %get-tuple-element.35) | copy-start | bytes 1179652
  25.0 26.7 %copy-start = (bf16[256,256]{1,0:T(8,128)(2,1)S(1)}, bf16[256,256]{1,0:T(8,128)(2,1)}, u32[]{:S(2)}) copy-start(bf16[256,256]{1,0:T(8,128)(2,1)} %constant.24.clone.refs_5_) | copy-start | bytes 393220
  25.0 26.7 %copy-start.2 = (bf16[8,16,2048]{2,1,0:T(8,128)(2,1)S(1)}, bf16[8,16,2048]{2,1,0:T(8,128)(2,1)}, u32[]{:S(2)}) copy-start(bf16[8,16,2048]{2,1,0:T(8,128)(2,1)} %get-tuple-element.39.refs_4_) | copy-start | bytes 1572868
  25.0 14.9 %collective-permute-start.4 = (bf16[16,16,2048]{2,1,0:T(8,128)(2,1)S(1)}, bf16[16,16,2048]{2,1,0:T(8,128)(2,1)S(1)}, u32[]{:S(2)}, u32[]{:S(2)}) collective-permute-start(bf16[16,16,2048]{2,1,0:T(8,128)(2,1)S(1)} %pad_maximum_fusion.refs_0_), channel_id=1, source_target_pairs={{0,2},{1,7},{2,4},{3,1},{4,6},{5,3},{6,0},{7,5},{8,10},{9,15},{10,... | collective-permute-start | bytes 3145736 | tf_op jit(solution)/shard_map/ppermute | solution.py:341
  30.4 27.6 %collective-permute-start.12 = (bf16[20,16,2048]{2,1,0:T(8,128)(2,1)S(1)}, bf16[20,16,2048]{2,1,0:T(8,128)(2,1)S(1)}, u32[]{:S(2)}, u32[]{:S(2)}) collective-permute-start(bf16[20,16,2048]{2,1,0:T(8,128)(2,1)S(1)} %constant_dynamic-update-slice_fusion.refs_0_), channel_id=1, source_target_pairs={{0,2},{1,7},{2,4},{3,1},{4,6},{5,3},{6,0},{7,5},{8,10},{9,15},{10,... | collective-permute-start | bytes 3932168 | tf_op jit(solution)/shard_map/ppermute | solution.py:341
  30.5 21.2 %collective-permute-start.3 = (bf16[16,16,2048]{2,1,0:T(8,128)(2,1)S(1)}, bf16[16,16,2048]{2,1,0:T(8,128)(2,1)S(1)}, u32[]{:S(2)}, u32[]{:S(2)}) collective-permute-start(bf16[16,16,2048]{2,1,0:T(8,128)(2,1)S(1)} %pad_maximum_fusion.refs_0_), channel_id=1, source_target_pairs={{0,1},{1,0},{2,3},{3,2},{4,5},{5,4},{6,7},{7,6},{8,9},{9,8},{10,11... | collective-permute-start | bytes 3145736 | tf_op jit(solution)/shard_map/ppermute | solution.py:344
  39.9 11.8 %collective-permute-start.7 = (bf16[16,16,2048]{2,1,0:T(8,128)(2,1)S(1)}, bf16[16,16,2048]{2,1,0:T(8,128)(2,1)S(1)}, u32[]{:S(2)}, u32[]{:S(2)}) collective-permute-start(bf16[16,16,2048]{2,1,0:T(8,128)(2,1)S(1)} %collective-permute-done.4.refs_2_), channel_id=1, source_target_pairs={{0,1},{1,0},{2,3},{3,2},{4,5},{5,4},{6,7},{7,6},{8,9},{9,8},{10,11... | collective-permute-start | bytes 3145736 | tf_op jit(solution)/shard_map/ppermute | solution.py:344
  45.8 14.0 %collective-permute-start.8 = (bf16[6,16,2048]{2,1,0:T(8,128)(2,1)S(1)}, bf16[6,16,2048]{2,1,0:T(8,128)(2,1)S(1)}, u32[]{:S(2)}, u32[]{:S(2)}) collective-permute-start(bf16[6,16,2048]{2,1,0:T(8,128)(2,1)S(1)} %copy-done.5), channel_id=1, source_target_pairs={{0,16},{1,121},{2,106},{3,3},{4,20},{5,125},{6,110},{7,7},{8,24},{... | collective-permute-start | bytes 1179656 | tf_op jit(solution)/shard_map/ppermute | solution.py:336
  51.6 8.8 %collective-permute-start.2 = (bf16[6,16,2048]{2,1,0:T(8,128)(2,1)S(1)}, bf16[6,16,2048]{2,1,0:T(8,128)(2,1)S(1)}, u32[]{:S(2)}, u32[]{:S(2)}) collective-permute-start(bf16[6,16,2048]{2,1,0:T(8,128)(2,1)S(1)} %copy-done.4), channel_id=1, source_target_pairs={{0,48},{1,81},{2,34},{3,67},{4,52},{5,85},{6,38},{7,71},{8,56},{9,... | collective-permute-start | bytes 1179656 | tf_op jit(solution)/shard_map/ppermute | solution.py:336
  51.6 11.1 %collective-permute-start.11 = (bf16[20,16,2048]{2,1,0:T(8,128)(2,1)S(1)}, bf16[20,16,2048]{2,1,0:T(8,128)(2,1)S(1)}, u32[]{:S(2)}, u32[]{:S(2)}) collective-permute-start(bf16[20,16,2048]{2,1,0:T(8,128)(2,1)S(1)} %constant_dynamic-update-slice_fusion.refs_0_), channel_id=1, source_target_pairs={{0,1},{1,0},{2,3},{3,2},{4,5},{5,4},{6,7},{7,6},{8,9},{9,8},{10,11... | collective-permute-start | bytes 3932168 | tf_op jit(solution)/shard_map/ppermute | solution.py:344
  58.0 4.8 %copy-start.1 = (bf16[10,16,2048]{2,1,0:T(8,128)(2,1)S(1)}, bf16[10,16,2048]{2,1,0:T(8,128)(2,1)}, u32[]{:S(2)}) copy-start(bf16[10,16,2048]{2,1,0:T(8,128)(2,1)} %get-tuple-element.45.refs_4_) | copy-start | bytes 1966084
  58.0 4.8 %collective-permute-start.13 = (bf16[20,16,2048]{2,1,0:T(8,128)(2,1)S(1)}, bf16[20,16,2048]{2,1,0:T(8,128)(2,1)S(1)}, u32[]{:S(2)}, u32[]{:S(2)}) collective-permute-start(bf16[20,16,2048]{2,1,0:T(8,128)(2,1)S(1)} %collective-permute-done.12.refs_2_), channel_id=1, source_target_pairs={{0,1},{1,0},{2,3},{3,2},{4,5},{5,4},{6,7},{7,6},{8,9},{9,8},{10,11... | collective-permute-start | bytes 3932168 | tf_op jit(solution)/shard_map/ppermute | solution.py:344
  60.4 11.2 %collective-permute-start.10 = (bf16[12,16,2048]{2,1,0:T(8,128)(2,1)S(1)}, bf16[12,16,2048]{2,1,0:T(8,128)(2,1)S(1)}, u32[]{:S(2)}, u32[]{:S(2)}) collective-permute-start(bf16[12,16,2048]{2,1,0:T(8,128)(2,1)S(1)} %constant_dynamic-update-slice_fusion.2.refs_0_), channel_id=1, source_target_pairs={{0,2},{1,7},{2,4},{3,1},{4,6},{5,3},{6,0},{7,5},{8,10},{9,15},{10,... | collective-permute-start | bytes 2359304 | tf_op jit(solution)/shard_map/ppermute | solution.py:341
  60.5 13.3 %collective-permute-start.9 = (bf16[12,16,2048]{2,1,0:T(8,128)(2,1)S(1)}, bf16[12,16,2048]{2,1,0:T(8,128)(2,1)S(1)}, u32[]{:S(2)}, u32[]{:S(2)}) collective-permute-start(bf16[12,16,2048]{2,1,0:T(8,128)(2,1)S(1)} %constant_dynamic-update-slice_fusion.2.refs_0_), channel_id=1, source_target_pairs={{0,1},{1,0},{2,3},{3,2},{4,5},{5,4},{6,7},{7,6},{8,9},{9,8},{10,11... | collective-permute-start | bytes 2359304 | tf_op jit(solution)/shard_map/ppermute | solution.py:344
  62.8 13.0 %copy-start.3 = (bf16[6,16,2048]{2,1,0:T(8,128)(2,1)S(1)}, bf16[6,16,2048]{2,1,0:T(8,128)(2,1)}, u32[]{:S(2)}) copy-start(bf16[6,16,2048]{2,1,0:T(8,128)(2,1)} %get-tuple-element.33.refs_4_) | copy-start | bytes 1179652
  71.6 4.1 %collective-permute-start.14 = (bf16[12,16,2048]{2,1,0:T(8,128)(2,1)S(1)}, bf16[12,16,2048]{2,1,0:T(8,128)(2,1)S(1)}, u32[]{:S(2)}, u32[]{:S(2)}) collective-permute-start(bf16[12,16,2048]{2,1,0:T(8,128)(2,1)S(1)} %collective-permute-done.10.refs_2_), channel_id=1, source_target_pairs={{0,1},{1,0},{2,3},{3,2},{4,5},{5,4},{6,7},{7,6},{8,9},{9,8},{10,11... | collective-permute-start | bytes 2359304 | tf_op jit(solution)/shard_map/ppermute | solution.py:344

commit v4 on v3

--- a/solution.py
+++ b/solution.py
@@ -318,6 +318,7 @@
 
 OTHER = pairs_of(lambda yl, z, yh, x, c: (yl, z, yh, x, 1 - c))
 ALONG = pairs_of(lambda yl, z, yh, x, c: (yl, z, yh, (x + 1 + 2 * c) % 4, c))
+BACK = pairs_of(lambda yl, z, yh, x, c: (yl, z, yh, (x + 3 - 2 * c) % 4, c))
 AXES = ("fsdp", "replica")
 
 
@@ -337,8 +338,8 @@
             for s, m in enumerate(sends)
         ]
 
-    def onward(message):
-        return lax.ppermute(message, AXES, ALONG)
+    def onward(message, pairs=ALONG):
+        return lax.ppermute(message, AXES, pairs)
 
     def swap(message):
         return lax.ppermute(message, AXES, OTHER)
@@ -355,17 +356,17 @@
     own0 = jnp.concatenate(own0)
     own0 = tied(own0, *picked[2])
     along0 = onward(own0)
-    other0 = swap(own0)
     own2 = fetch(2, [tied(m, own0) for m in picked[2][:2]])
     own1 = jnp.concatenate(own1)
     along1 = onward(own1)
+    other0 = swap(own0)
     other1 = swap(own1)
-    along_other0 = swap(tied(along0, own1))
+    along_other0 = swap(tied(along0, *own2))
     done = turn(0, [own0, other0, along0, along_other0], done)
+    own2 = jnp.concatenate([tied(m, done[2]) for m in own2])
+    along2 = onward(own2, BACK)
+    other2 = swap(own2)
     along_other1 = swap(tied(along1, done[2]))
-    own2 = jnp.concatenate([tied(m, done[2]) for m in own2])
-    along2 = onward(own2)
-    other2 = swap(own2)
     done = turn(1, [own1, other1, along1, along_other1], done)
     along_other2 = swap(tied(along2, done[2]))
     done = turn(2, [own2, other2, along2, along_other2], done)

time: 81.2 us -> 79.7 us (0.982)
  starting transfers between devices: 41.5 us -> 39.4 us
    ppermute x6, waiting for transfers between devices: 5.63 us -> 0.02 us  [fetch(): lax.ppermute(m, AXES, fetch_pairs(s, FLIPPED[k]))]
    ppermute x6, waiting for transfers between devices: 1.92 us -> 6.73 us  [swap(): return lax.ppermute(message, AXES, OTHER)]
    ppermute x6, starting transfers between devices: 21.8 us -> 20.3 us  [swap(): return lax.ppermute(message, AXES, OTHER)]
  transfers between devices with their start and end apart: 15 -> 15, of which waited for: 5 -> 4; matrix products, arithmetic and copies ran while one was open for 0% -> 0% of each run, Pallas kernels for 26% -> 27%
where the time goes in v4:
time: 79.7 us; the launch traced here: 79.2 us
  starting transfers between devices  39.4 us (49%)
  Pallas kernels  29.3 us (37%)
  waiting for transfers between devices  8.63 us (11%)
  local copies, waits for them, and re-layouts  0.92 us (1%)
  between operations  0.87 us (1%)
    ppermute x6, starting transfers between devices, swap(): return lax.ppermute(message, AXES, OTHER)  20.3 us
    ppermute x6, starting transfers between devices, fetch(): lax.ppermute(m, AXES, fetch_pairs(s, FLIPPED[k]))  18.9 us
    pallas_call x3, Pallas kernels, rotate(): pl.pallas_call(functools.partial(rotate_kernel, part, len(aliases)), grid...  18.7 us
    pallas_call x3, Pallas kernels, pick(): pl.pallas_call(functools.partial(pick_kernel, part), grid_spec=pltpu.Pref...  10.6 us
    ppermute x6, waiting for transfers between devices, swap(): return lax.ppermute(message, AXES, OTHER)  6.73 us
    ppermute x3, waiting for transfers between devices, onward(): return lax.ppermute(message, AXES, pairs)  1.88 us
  transfers between devices with their start and end apart: 15, of which 4 were waited for; matrix products, arithmetic and copies ran while one was open for 0% of the time, Pallas kernels for 27%

profile of v4, /device:TPU:1, one launch (start us, length us, event | category | flops | bytes accessed | tf_op | source)
XLA Modules:
  0.0 79.2 jit_solution(15874624327914140646)
XLA Ops:
  0.6 3.2 %pick_rows.4 = (bf16[8,16,2048]{2,1,0:T(8,128)(2,1)}, bf16[8,16,2048]{2,1,0:T(8,128)(2,1)}, bf16[8,16,2048]{2,1,0:T(8,128)(2,1)}) custom-call(s32[16]{0:T(128)} %share.5, s32[8]{0:T(128)} %ranks.5, s32[1]{0:T(128)} %bitcast.f_ref, s32[1]{0:T(128)} %bitcast.1.r_ref, bf16[2,512,2048]{2,1,0:T(8,128)(2,1)} %out_hbm.5, bf16[2,1024,2048]{2,1,0:T(8,128)(2,1)} %down_hbm.5), custom_call_target="tpu_custom_call" | custom-call | bytes 4718592 | tf_op jit(solution)/shard_map/pick_rows/pallas_call | solution.py:124
  3.8 3.5 %collective-permute-start = (bf16[8,16,2048]{2,1,0:T(8,128)(2,1)}, bf16[8,16,2048]{2,1,0:T(8,128)(2,1)S(1)}, u32[]{:S(2)}, u32[]{:S(2)}) collective-permute-start(bf16[8,16,2048]{2,1,0:T(8,128)(2,1)} %get-tuple-element.30), channel_id=1, source_target_pairs={{0,48},{1,81},{2,34},{3,67},{4,52},{5,85},{6,38},{7,71},{8,56},{9,... | collective-permute-start | bytes 1572872 | tf_op jit(solution)/shard_map/ppermute | solution.py:337
  7.4 5.5 %collective-permute-start.1 = (bf16[8,16,2048]{2,1,0:T(8,128)(2,1)}, bf16[8,16,2048]{2,1,0:T(8,128)(2,1)S(1)}, u32[]{:S(2)}, u32[]{:S(2)}) collective-permute-start(bf16[8,16,2048]{2,1,0:T(8,128)(2,1)} %get-tuple-element.31), channel_id=1, source_target_pairs={{0,16},{1,121},{2,106},{3,3},{4,20},{5,125},{6,110},{7,7},{8,24},{... | collective-permute-start | bytes 1572872 | tf_op jit(solution)/shard_map/ppermute | solution.py:337
  12.9 3.6 %pick_rows.5 = (bf16[10,16,2048]{2,1,0:T(8,128)(2,1)}, bf16[10,16,2048]{2,1,0:T(8,128)(2,1)}, bf16[10,16,2048]{2,1,0:T(8,128)(2,1)}) custom-call(s32[16]{0:T(128)} %share.5, s32[8]{0:T(128)} %ranks.5, s32[1]{0:T(128)} %bitcast.f_ref, s32[1]{0:T(128)} %bitcast.1.r_ref, bf16[2,512,2048]{2,1,0:T(8,128)(2,1)} %out_hbm.5, bf16[2,1024,2048]{2,1,0:T(8,128)(2,1)} %down_hbm.5), custom_call_target="tpu_custom_call" | custom-call | bytes 5898240 | tf_op jit(solution)/shard_map/pick_rows/pallas_call | solution.py:124
  16.5 0.1 collective-permute-start.9
  16.6 4.6 %collective-permute-start.10 = (bf16[10,16,2048]{2,1,0:T(8,128)(2,1)}, bf16[10,16,2048]{2,1,0:T(8,128)(2,1)S(1)}, u32[]{:S(2)}, u32[]{:S(2)}) collective-permute-start(bf16[10,16,2048]{2,1,0:T(8,128)(2,1)} %get-tuple-element.43), channel_id=1, source_target_pairs={{0,16},{1,121},{2,106},{3,3},{4,20},{5,125},{6,110},{7,7},{8,24},{... | collective-permute-start | bytes 1966088 | tf_op jit(solution)/shard_map/ppermute | solution.py:337
  21.2 3.8 %pick_rows.3 = (bf16[6,16,2048]{2,1,0:T(8,128)(2,1)}, bf16[6,16,2048]{2,1,0:T(8,128)(2,1)}, bf16[6,16,2048]{2,1,0:T(8,128)(2,1)}) custom-call(s32[16]{0:T(128)} %share.5, s32[8]{0:T(128)} %ranks.5, s32[1]{0:T(128)} %bitcast.f_ref, s32[1]{0:T(128)} %bitcast.1.r_ref, bf16[2,512,2048]{2,1,0:T(8,128)(2,1)} %out_hbm.5, bf16[2,1024,2048]{2,1,0:T(8,128)(2,1)} %down_hbm.5), custom_call_target="tpu_custom_call" | custom-call | bytes 3538944 | tf_op jit(solution)/shard_map/pick_rows/pallas_call | solution.py:124
  25.0 0.0 collective-permute-done
  25.1 0.1 pad_maximum_fusion.refs_0_
  25.2 0.0 copy-start
  25.2 0.1 collective-permute-start.4
  25.3 0.7 copy-done.5
  26.0 4.5 %collective-permute-start.5 = (bf16[6,16,2048]{2,1,0:T(8,128)(2,1)S(1)}, bf16[6,16,2048]{2,1,0:T(8,128)(2,1)S(1)}, u32[]{:S(2)}, u32[]{:S(2)}) collective-permute-start(bf16[6,16,2048]{2,1,0:T(8,128)(2,1)S(1)} %copy-done.5), channel_id=1, source_target_pairs={{0,16},{1,121},{2,106},{3,3},{4,20},{5,125},{6,110},{7,7},{8,24},{... | collective-permute-start | bytes 1179656 | tf_op jit(solution)/shard_map/ppermute | solution.py:337
  30.5 0.7 collective-permute-start.2
  31.2 0.0 collective-permute-done.9
  31.2 0.0 collective-permute-done.10
  31.3 0.1 collective-permute-start.12
  31.4 9.7 %collective-permute-start.3 = (bf16[16,16,2048]{2,1,0:T(8,128)(2,1)S(1)}, bf16[16,16,2048]{2,1,0:T(8,128)(2,1)S(1)}, u32[]{:S(2)}, u32[]{:S(2)}) collective-permute-start(bf16[16,16,2048]{2,1,0:T(8,128)(2,1)S(1)} %pad_maximum_fusion.refs_0_), channel_id=1, source_target_pairs={{0,1},{1,0},{2,3},{3,2},{4,5},{5,4},{6,7},{7,6},{8,9},{9,8},{10,11... | collective-permute-start | bytes 3145736 | tf_op jit(solution)/shard_map/ppermute | solution.py:345
  41.1 0.0 collective-permute-done.5
  41.1 0.0 collective-permute-done.2
  41.1 4.7 %collective-permute-start.6 = (bf16[16,16,2048]{2,1,0:T(8,128)(2,1)S(1)}, bf16[16,16,2048]{2,1,0:T(8,128)(2,1)S(1)}, u32[]{:S(2)}, u32[]{:S(2)}) collective-permute-start(bf16[16,16,2048]{2,1,0:T(8,128)(2,1)S(1)} %collective-permute-done.4.refs_2_), channel_id=1, source_target_pairs={{0,1},{1,0},{2,3},{3,2},{4,5},{5,4},{6,7},{7,6},{8,9},{9,8},{10,11... | collective-permute-start | bytes 3145736 | tf_op jit(solution)/shard_map/ppermute | solution.py:345
  45.8 0.0 collective-permute-start.11
  45.8 2.3 %collective-permute-done.6.refs_3_ = bf16[16,16,2048]{2,1,0:T(8,128)(2,1)S(1)} collective-permute-done((bf16[16,16,2048]{2,1,0:T(8,128)(2,1)S(1)}, bf16[16,16,2048]{2,1,0:T(8,128)(2,1)S(1)}, u32[]{:S(2)}, u32[]{:S(2)}) %collective-permute-start.6) | collective-permute-done | bytes 1048608 | tf_op jit(solution)/shard_map/ppermute | solution.py:345
  48.1 6.2 %rotate_cast.3 = (bf16[256,16384]{1,0:T(8,128)(2,1)}, bf16[256,128]{1,0:T(8,128)(2,1)}) custom-call(s32[1]{0:T(128)} %bitcast.f_ref, s32[1]{0:T(128)} %bitcast.1.r_ref, bf16[16,16,2048]{2,1,0:T(8,128)(2,1)S(1)} %pad_maximum_fusion.refs_0_, bf16[16,16,2048]{2,1,0:T(8,128)(2,1)S(1)} %collective-permute-done.3.refs_1_, ...), custom_call_target="tpu_custom_call" | custom-call | flops 536870912 | bytes 8388608 | tf_op jit(solution)/shard_map/rotate_cast/pallas_call | solution.py:271
  54.3 5.5 %collective-permute-start.13 = (bf16[20,16,2048]{2,1,0:T(8,128)(2,1)S(1)}, bf16[20,16,2048]{2,1,0:T(8,128)(2,1)S(1)}, u32[]{:S(2)}, u32[]{:S(2)}) collective-permute-start(bf16[20,16,2048]{2,1,0:T(8,128)(2,1)S(1)} %collective-permute-done.12.refs_2_), channel_id=1, source_target_pairs={{0,1},{1,0},{2,3},{3,2},{4,5},{5,4},{6,7},{7,6},{8,9},{9,8},{10,11... | collective-permute-start | bytes 3932168 | tf_op jit(solution)/shard_map/ppermute | solution.py:345
  59.9 0.1 collective-permute-start.8
  60.0 0.3 collective-permute-start.7
  60.4 2.2 %collective-permute-done.13.refs_3_ = bf16[20,16,2048]{2,1,0:T(8,128)(2,1)S(1)} collective-permute-done((bf16[20,16,2048]{2,1,0:T(8,128)(2,1)S(1)}, bf16[20,16,2048]{2,1,0:T(8,128)(2,1)S(1)}, u32[]{:S(2)}, u32[]{:S(2)}) %collective-permute-start.13) | collective-permute-done | bytes 1310752 | tf_op jit(solution)/shard_map/ppermute | solution.py:345
  62.5 7.6 %rotate_cast.4 = (bf16[256,16384]{1,0:T(8,128)(2,1)}, bf16[256,128]{1,0:T(8,128)(2,1)}, bf16[128,16384]{1,0:T(8,128)(2,1)}, bf16[128,128]{1,0:T(8,128)(2,1)}) custom-call(s32[1]{0:T(128)} %bitcast.f_ref, s32[1]{0:T(128)} %bitcast.1.r_ref, ...), custom_call_target="tpu_custom_call", output_to_operand_aliasing={{0}: (8, {}), {1}: (9, {})} | custom-call | flops 671088640 | bytes 10485760 | tf_op jit(solution)/shard_map/rotate_cast/pallas_call | solution.py:271
  70.2 1.9 %collective-permute-done.8.refs_2_ = bf16[12,16,2048]{2,1,0:T(8,128)(2,1)S(1)} collective-permute-done((bf16[12,16,2048]{2,1,0:T(8,128)(2,1)S(1)}, bf16[12,16,2048]{2,1,0:T(8,128)(2,1)S(1)}, u32[]{:S(2)}, u32[]{:S(2)}) %collective-permute-start.8) | collective-permute-done | bytes 786464 | tf_op jit(solution)/shard_map/ppermute | solution.py:342
  72.1 2.3 %collective-permute-done.14.refs_3_ = bf16[12,16,2048]{2,1,0:T(8,128)(2,1)S(1)} collective-permute-done((bf16[12,16,2048]{2,1,0:T(8,128)(2,1)S(1)}, bf16[12,16,2048]{2,1,0:T(8,128)(2,1)S(1)}, u32[]{:S(2)}, u32[]{:S(2)}) %collective-permute-start.14) | collective-permute-done | bytes 786464 | tf_op jit(solution)/shard_map/ppermute | solution.py:345
  74.3 4.9 %rotate_cast.5 = (bf16[128,16384]{1,0:T(8,128)(2,1)}, bf16[128,128]{1,0:T(8,128)(2,1)}) custom-call(s32[1]{0:T(128)} %bitcast.f_ref, s32[1]{0:T(128)} %bitcast.1.r_ref, bf16[12,16,2048]{2,1,0:T(8,128)(2,1)S(1)} %constant_dynamic-update-slice_fusion.refs_0_, ...), custom_call_target="tpu_custom_call", output_to_operand_aliasing={{0}: (8, {}), {1}: (9, {})} | custom-call | flops 402653184 | bytes 6291456 | tf_op jit(solution)/shard_map/rotate_cast/pallas_call | solution.py:271
  (21 shorter events, 0.2 us)
Async XLA Ops:
  3.8 21.2 %collective-permute-start = (bf16[8,16,2048]{2,1,0:T(8,128)(2,1)}, bf16[8,16,2048]{2,1,0:T(8,128)(2,1)S(1)}, u32[]{:S(2)}, u32[]{:S(2)}) collective-permute-start(bf16[8,16,2048]{2,1,0:T(8,128)(2,1)} %get-tuple-element.30), channel_id=1, source_target_pairs={{0,48},{1,81},{2,34},{3,67},{4,52},{5,85},{6,38},{7,71},{8,56},{9,... | collective-permute-start | bytes 1572872 | tf_op jit(solution)/shard_map/ppermute | solution.py:337
  7.4 17.7 %collective-permute-start.1 = (bf16[8,16,2048]{2,1,0:T(8,128)(2,1)}, bf16[8,16,2048]{2,1,0:T(8,128)(2,1)S(1)}, u32[]{:S(2)}, u32[]{:S(2)}) collective-permute-start(bf16[8,16,2048]{2,1,0:T(8,128)(2,1)} %get-tuple-element.31), channel_id=1, source_target_pairs={{0,16},{1,121},{2,106},{3,3},{4,20},{5,125},{6,110},{7,7},{8,24},{... | collective-permute-start | bytes 1572872 | tf_op jit(solution)/shard_map/ppermute | solution.py:337
  16.5 14.7 %collective-permute-start.9 = (bf16[10,16,2048]{2,1,0:T(8,128)(2,1)}, bf16[10,16,2048]{2,1,0:T(8,128)(2,1)S(1)}, u32[]{:S(2)}, u32[]{:S(2)}) collective-permute-start(bf16[10,16,2048]{2,1,0:T(8,128)(2,1)} %get-tuple-element.42), channel_id=1, source_target_pairs={{0,48},{1,81},{2,34},{3,67},{4,52},{5,85},{6,38},{7,71},{8,56},{9,... | collective-permute-start | bytes 1966088 | tf_op jit(solution)/shard_map/ppermute | solution.py:337
  16.6 14.7 %collective-permute-start.10 = (bf16[10,16,2048]{2,1,0:T(8,128)(2,1)}, bf16[10,16,2048]{2,1,0:T(8,128)(2,1)S(1)}, u32[]{:S(2)}, u32[]{:S(2)}) collective-permute-start(bf16[10,16,2048]{2,1,0:T(8,128)(2,1)} %get-tuple-element.43), channel_id=1, source_target_pairs={{0,16},{1,121},{2,106},{3,3},{4,20},{5,125},{6,110},{7,7},{8,24},{... | collective-permute-start | bytes 1966088 | tf_op jit(solution)/shard_map/ppermute | solution.py:337
  25.0 1.0 %copy-start.5 = (bf16[6,16,2048]{2,1,0:T(8,128)(2,1)S(1)}, bf16[6,16,2048]{2,1,0:T(8,128)(2,1)}, u32[]{:S(2)}) copy-start(bf16[6,16,2048]{2,1,0:T(8,128)(2,1)} %get-tuple-element.36) | copy-start | bytes 1179652
  25.0 5.5 %copy-start.4 = (bf16[6,16,2048]{2,1,0:T(8,128)(2,1)S(1)}, bf16[6,16,2048]{2,1,0:T(8,128)(2,1)}, u32[]{:S(2)}) copy-start(bf16[6,16,2048]{2,1,0:T(8,128)(2,1)} %get-tuple-element.35) | copy-start | bytes 1179652
  25.2 22.9 %copy-start = (bf16[256,256]{1,0:T(8,128)(2,1)S(1)}, bf16[256,256]{1,0:T(8,128)(2,1)}, u32[]{:S(2)}) copy-start(bf16[256,256]{1,0:T(8,128)(2,1)} %constant.24.clone.refs_5_) | copy-start | bytes 393220
  25.2 22.9 %copy-start.2 = (bf16[8,16,2048]{2,1,0:T(8,128)(2,1)S(1)}, bf16[8,16,2048]{2,1,0:T(8,128)(2,1)}, u32[]{:S(2)}) copy-start(bf16[8,16,2048]{2,1,0:T(8,128)(2,1)} %get-tuple-element.38.refs_4_) | copy-start | bytes 1572868
  25.2 15.9 %collective-permute-start.4 = (bf16[16,16,2048]{2,1,0:T(8,128)(2,1)S(1)}, bf16[16,16,2048]{2,1,0:T(8,128)(2,1)S(1)}, u32[]{:S(2)}, u32[]{:S(2)}) collective-permute-start(bf16[16,16,2048]{2,1,0:T(8,128)(2,1)S(1)} %pad_maximum_fusion.refs_0_), channel_id=1, source_target_pairs={{0,2},{1,7},{2,4},{3,1},{4,6},{5,3},{6,0},{7,5},{8,10},{9,15},{10,... | collective-permute-start | bytes 3145736 | tf_op jit(solution)/shard_map/ppermute | solution.py:342
  26.0 15.1 %collective-permute-start.5 = (bf16[6,16,2048]{2,1,0:T(8,128)(2,1)S(1)}, bf16[6,16,2048]{2,1,0:T(8,128)(2,1)S(1)}, u32[]{:S(2)}, u32[]{:S(2)}) collective-permute-start(bf16[6,16,2048]{2,1,0:T(8,128)(2,1)S(1)} %copy-done.5), channel_id=1, source_target_pairs={{0,16},{1,121},{2,106},{3,3},{4,20},{5,125},{6,110},{7,7},{8,24},{... | collective-permute-start | bytes 1179656 | tf_op jit(solution)/shard_map/ppermute | solution.py:337
  30.5 10.5 %collective-permute-start.2 = (bf16[6,16,2048]{2,1,0:T(8,128)(2,1)S(1)}, bf16[6,16,2048]{2,1,0:T(8,128)(2,1)S(1)}, u32[]{:S(2)}, u32[]{:S(2)}) collective-permute-start(bf16[6,16,2048]{2,1,0:T(8,128)(2,1)S(1)} %copy-done.4), channel_id=1, source_target_pairs={{0,48},{1,81},{2,34},{3,67},{4,52},{5,85},{6,38},{7,71},{8,56},{9,... | collective-permute-start | bytes 1179656 | tf_op jit(solution)/shard_map/ppermute | solution.py:337
  31.3 23.0 %collective-permute-start.12 = (bf16[20,16,2048]{2,1,0:T(8,128)(2,1)S(1)}, bf16[20,16,2048]{2,1,0:T(8,128)(2,1)S(1)}, u32[]{:S(2)}, u32[]{:S(2)}) collective-permute-start(bf16[20,16,2048]{2,1,0:T(8,128)(2,1)S(1)} %constant_dynamic-update-slice_fusion.2.refs_0_), channel_id=1, source_target_pairs={{0,2},{1,7},{2,4},{3,1},{4,6},{5,3},{6,0},{7,5},{8,10},{9,15},{10,... | collective-permute-start | bytes 3932168 | tf_op jit(solution)/shard_map/ppermute | solution.py:342
  31.4 14.4 %collective-permute-start.3 = (bf16[16,16,2048]{2,1,0:T(8,128)(2,1)S(1)}, bf16[16,16,2048]{2,1,0:T(8,128)(2,1)S(1)}, u32[]{:S(2)}, u32[]{:S(2)}) collective-permute-start(bf16[16,16,2048]{2,1,0:T(8,128)(2,1)S(1)} %pad_maximum_fusion.refs_0_), channel_id=1, source_target_pairs={{0,1},{1,0},{2,3},{3,2},{4,5},{5,4},{6,7},{7,6},{8,9},{9,8},{10,11... | collective-permute-start | bytes 3145736 | tf_op jit(solution)/shard_map/ppermute | solution.py:345
  41.1 7.0 %collective-permute-start.6 = (bf16[16,16,2048]{2,1,0:T(8,128)(2,1)S(1)}, bf16[16,16,2048]{2,1,0:T(8,128)(2,1)S(1)}, u32[]{:S(2)}, u32[]{:S(2)}) collective-permute-start(bf16[16,16,2048]{2,1,0:T(8,128)(2,1)S(1)} %collective-permute-done.4.refs_2_), channel_id=1, source_target_pairs={{0,1},{1,0},{2,3},{3,2},{4,5},{5,4},{6,7},{7,6},{8,9},{9,8},{10,11... | collective-permute-start | bytes 3145736 | tf_op jit(solution)/shard_map/ppermute | solution.py:345
  45.8 14.5 %collective-permute-start.11 = (bf16[20,16,2048]{2,1,0:T(8,128)(2,1)S(1)}, bf16[20,16,2048]{2,1,0:T(8,128)(2,1)S(1)}, u32[]{:S(2)}, u32[]{:S(2)}) collective-permute-start(bf16[20,16,2048]{2,1,0:T(8,128)(2,1)S(1)} %constant_dynamic-update-slice_fusion.2.refs_0_), channel_id=1, source_target_pairs={{0,1},{1,0},{2,3},{3,2},{4,5},{5,4},{6,7},{7,6},{8,9},{9,8},{10,11... | collective-permute-start | bytes 3932168 | tf_op jit(solution)/shard_map/ppermute | solution.py:345
  54.3 8.2 %copy-start.1 = (bf16[10,16,2048]{2,1,0:T(8,128)(2,1)S(1)}, bf16[10,16,2048]{2,1,0:T(8,128)(2,1)}, u32[]{:S(2)}) copy-start(bf16[10,16,2048]{2,1,0:T(8,128)(2,1)} %get-tuple-element.45.refs_4_) | copy-start | bytes 1966084
  54.3 8.2 %collective-permute-start.13 = (bf16[20,16,2048]{2,1,0:T(8,128)(2,1)S(1)}, bf16[20,16,2048]{2,1,0:T(8,128)(2,1)S(1)}, u32[]{:S(2)}, u32[]{:S(2)}) collective-permute-start(bf16[20,16,2048]{2,1,0:T(8,128)(2,1)S(1)} %collective-permute-done.12.refs_2_), channel_id=1, source_target_pairs={{0,1},{1,0},{2,3},{3,2},{4,5},{5,4},{6,7},{7,6},{8,9},{9,8},{10,11... | collective-permute-start | bytes 3932168 | tf_op jit(solution)/shard_map/ppermute | solution.py:345
  59.9 12.1 %collective-permute-start.8 = (bf16[12,16,2048]{2,1,0:T(8,128)(2,1)S(1)}, bf16[12,16,2048]{2,1,0:T(8,128)(2,1)S(1)}, u32[]{:S(2)}, u32[]{:S(2)}) collective-permute-start(bf16[12,16,2048]{2,1,0:T(8,128)(2,1)S(1)} %constant_dynamic-update-slice_fusion.refs_0_), channel_id=1, source_target_pairs={{0,6},{1,3},{2,0},{3,5},{4,2},{5,7},{6,4},{7,1},{8,14},{9,11},{10,... | collective-permute-start | bytes 2359304 | tf_op jit(solution)/shard_map/ppermute | solution.py:342
  60.0 12.0 %collective-permute-start.7 = (bf16[12,16,2048]{2,1,0:T(8,128)(2,1)S(1)}, bf16[12,16,2048]{2,1,0:T(8,128)(2,1)S(1)}, u32[]{:S(2)}, u32[]{:S(2)}) collective-permute-start(bf16[12,16,2048]{2,1,0:T(8,128)(2,1)S(1)} %constant_dynamic-update-slice_fusion.refs_0_), channel_id=1, source_target_pairs={{0,1},{1,0},{2,3},{3,2},{4,5},{5,4},{6,7},{7,6},{8,9},{9,8},{10,11... | collective-permute-start | bytes 2359304 | tf_op jit(solution)/shard_map/ppermute | solution.py:345
  62.5 11.8 %copy-start.3 = (bf16[6,16,2048]{2,1,0:T(8,128)(2,1)S(1)}, bf16[6,16,2048]{2,1,0:T(8,128)(2,1)}, u32[]{:S(2)}) copy-start(bf16[6,16,2048]{2,1,0:T(8,128)(2,1)} %get-tuple-element.33.refs_4_) | copy-start | bytes 1179652
  72.0 2.3 %collective-permute-start.14 = (bf16[12,16,2048]{2,1,0:T(8,128)(2,1)S(1)}, bf16[12,16,2048]{2,1,0:T(8,128)(2,1)S(1)}, u32[]{:S(2)}, u32[]{:S(2)}) collective-permute-start(bf16[12,16,2048]{2,1,0:T(8,128)(2,1)S(1)} %collective-permute-done.8.refs_2_), channel_id=1, source_target_pairs={{0,1},{1,0},{2,3},{3,2},{4,5},{5,4},{6,7},{7,6},{8,9},{9,8},{10,11... | collective-permute-start | bytes 2359304 | tf_op jit(solution)/shard_map/ppermute | solution.py:345

commit v5 on v4

--- a/solution.py
+++ b/solution.py
@@ -65,14 +65,15 @@
     return ((here // 4) ^ dy) * 4 + ((here + dz) & 3)
 
 
-def pick_kernel(part, share, ranks, f_ref, r_ref, out_hbm, down_hbm, *refs):
+def pick_kernel(part, which, share, ranks, f_ref, r_ref, out_hbm, down_hbm, *refs):
     o0, no, d0, nd = part
     n = no + nd
-    sends, (pairs, stage, sems, gone) = refs[:3], refs[3:]
+    kinds = len(which)
+    sends, (pairs, stage, sems, gone) = refs[:kinds], refs[kinds:]
     here, role = f_ref[0], r_ref[0]
-    to = [shard_at(here, role, slot, True) for slot in range(2)] + [here]
+    to = [shard_at(here, role, slot, True) if slot < 2 else here for slot in which]
     copies = []
-    for i in range(3):
+    for i in range(kinds):
         rank = ranks[to[i]]
         mine = []
         for u in range(no):
@@ -100,7 +101,7 @@
             c.start()
         copies.append(mine)
     leaving = []
-    for i in range(3):
+    for i in range(kinds):
         for c in copies[i]:
             c.wait()
         for u in range(no):
@@ -117,25 +118,26 @@
         c.wait()
 
 
-def pick(part, share, ranks, here, role, out_weight, down_weight):
+def pick(part, which, share, ranks, here, role, out_weight, down_weight):
     o0, no, d0, nd = part
     n = no + nd
     shape = (n, UNIT, LOCAL)
+    kinds = len(which)
     return pl.pallas_call(
-        functools.partial(pick_kernel, part),
+        functools.partial(pick_kernel, part, which),
         grid_spec=pltpu.PrefetchScalarGridSpec(
             num_scalar_prefetch=4,
             grid=(),
             in_specs=[pl.BlockSpec(memory_space=pltpu.HBM)] * 2,
-            out_specs=[pl.BlockSpec(memory_space=pltpu.HBM)] * 3,
+            out_specs=[pl.BlockSpec(memory_space=pltpu.HBM)] * kinds,
             scratch_shapes=[
-                pltpu.VMEM((3, max(no, 1), 2, UNIT, LOCAL), jnp.bfloat16),
-                pltpu.VMEM((3,) + shape, jnp.bfloat16),
-                pltpu.SemaphoreType.DMA((3, 2 * no + nd)),
-                pltpu.SemaphoreType.DMA((3,)),
+                pltpu.VMEM((kinds, max(no, 1), 2, UNIT, LOCAL), jnp.bfloat16),
+                pltpu.VMEM((kinds,) + shape, jnp.bfloat16),
+                pltpu.SemaphoreType.DMA((kinds, 2 * no + nd)),
+                pltpu.SemaphoreType.DMA((kinds,)),
             ],
         ),
-        out_shape=[jax.ShapeDtypeStruct(shape, jnp.bfloat16)] * 3,
+        out_shape=[jax.ShapeDtypeStruct(shape, jnp.bfloat16)] * kinds,
         compiler_params=pltpu.CompilerParams(vmem_limit_bytes=VMEM),
         cost_estimate=pl.CostEstimate(
             flops=0, bytes_accessed=9 * math.prod(shape) * 2, transcendentals=0
@@ -327,10 +329,17 @@
     seat = (lax.axis_index("replica") % 4).astype(jnp.int32)[None]
     roles = [seat ^ 2 * f for f in FLIPPED]
     rot = two_blocks()
-    picked = [
-        pick(part, layer_share, rank_map, here, role, out_weight, down_weight)
-        for part, role in zip(PARTS, roles)
-    ]
+
+    def choose(k, which):
+        return list(
+            pick(
+                PARTS[k], which, layer_share, rank_map, here, roles[k], out_weight,
+                down_weight,
+            )
+        )
+
+    picked = [choose(0, (0, 1)), choose(1, (0, 1, 2)), choose(2, (0, 1, 2))]
+    picked[0] += choose(0, (2,))
 
     def fetch(k, sends):
         return [
@@ -354,7 +363,7 @@
     own0 = fetch(0, picked[0][:2])
     own1 = fetch(1, picked[1][:2])
     own0 = jnp.concatenate(own0)
-    own0 = tied(own0, *picked[2])
+    own0 = tied(own0, *picked[2], picked[0][2])
     along0 = onward(own0)
     own2 = fetch(2, [tied(m, own0) for m in picked[2][:2]])
     own1 = jnp.concatenate(own1)

time: 79.7 us -> 79.6 us (level)
  starting transfers between devices: 39.4 us -> 35.1 us
  Pallas kernels: 29.3 us -> 31.5 us
  waiting for transfers between devices: 8.63 us -> 10.5 us
    ppermute x6, starting transfers between devices: 20.3 us -> 16 us  [swap(): return lax.ppermute(message, AXES, OTHER)]
    pallas_call x3 -> x4, Pallas kernels: 10.6 us -> 12.8 us  [pick(): pl.pallas_call(functools.partial(pick_kernel, part, which), grid_spec=plt...]
    ppermute x6, waiting for transfers between devices: 0.02 us -> 1.37 us  [fetch(): lax.ppermute(m, AXES, fetch_pairs(s, FLIPPED[k]))]
    ppermute x3, waiting for transfers between devices: 1.88 us -> 3.15 us  [onward(): return lax.ppermute(message, AXES, pairs)]
  transfers between devices with their start and end apart: 15 -> 15, of which waited for: 4 -> 6; matrix products, arithmetic and copies ran while one was open for 0% -> 0% of each run, Pallas kernels for 27% -> 30%
where the time goes in v5:
time: 79.6 us; the launch traced here: 79 us
  starting transfers between devices  35.1 us (44%)
  Pallas kernels  31.5 us (40%)
  waiting for transfers between devices  10.5 us (13%)
  local copies, waits for them, and re-layouts  0.92 us (1%)
  between operations  0.86 us (1%)
    ppermute x6, starting transfers between devices, fetch(): lax.ppermute(m, AXES, fetch_pairs(s, FLIPPED[k]))  18.9 us
    pallas_call x3, Pallas kernels, rotate(): pl.pallas_call(functools.partial(rotate_kernel, part, len(aliases)), grid...  18.7 us
    ppermute x6, starting transfers between devices, swap(): return lax.ppermute(message, AXES, OTHER)  16 us
    pallas_call x4, Pallas kernels, pick(): pl.pallas_call(functools.partial(pick_kernel, part, which), grid_spec=plt...  12.8 us
    ppermute x6, waiting for transfers between devices, swap(): return lax.ppermute(message, AXES, OTHER)  6.02 us
    ppermute x3, waiting for transfers between devices, onward(): return lax.ppermute(message, AXES, pairs)  3.15 us
  transfers between devices with their start and end apart: 15, of which 6 were waited for; matrix products, arithmetic and copies ran while one was open for 0% of the time, Pallas kernels for 30%

profile of v5, /device:TPU:1, one launch (start us, length us, event | category | flops | bytes accessed | tf_op | source)
XLA Modules:
  0.0 79.0 jit_solution(6802851462860239974)
XLA Ops:
  0.6 2.9 %pick_rows.5 = (bf16[8,16,2048]{2,1,0:T(8,128)(2,1)}, bf16[8,16,2048]{2,1,0:T(8,128)(2,1)}) custom-call(s32[16]{0:T(128)} %share.7, s32[8]{0:T(128)} %ranks.7, s32[1]{0:T(128)} %bitcast.f_ref, s32[1]{0:T(128)} %bitcast.1.r_ref, bf16[2,512,2048]{2,1,0:T(8,128)(2,1)} %out_hbm.7, bf16[2,1024,2048]{2,1,0:T(8,128)(2,1)} %down_hbm.7), custom_call_target="tpu_custom_call" | custom-call | bytes 4718592 | tf_op jit(solution)/shard_map/pick_rows/pallas_call | solution.py:126
  3.6 3.5 %collective-permute-start = (bf16[8,16,2048]{2,1,0:T(8,128)(2,1)}, bf16[8,16,2048]{2,1,0:T(8,128)(2,1)S(1)}, u32[]{:S(2)}, u32[]{:S(2)}) collective-permute-start(bf16[8,16,2048]{2,1,0:T(8,128)(2,1)} %get-tuple-element.29), channel_id=1, source_target_pairs={{0,48},{1,81},{2,34},{3,67},{4,52},{5,85},{6,38},{7,71},{8,56},{9,... | collective-permute-start | bytes 1572872 | tf_op jit(solution)/shard_map/ppermute | solution.py:346
  7.1 5.5 %collective-permute-start.1 = (bf16[8,16,2048]{2,1,0:T(8,128)(2,1)}, bf16[8,16,2048]{2,1,0:T(8,128)(2,1)S(1)}, u32[]{:S(2)}, u32[]{:S(2)}) collective-permute-start(bf16[8,16,2048]{2,1,0:T(8,128)(2,1)} %get-tuple-element.30), channel_id=1, source_target_pairs={{0,16},{1,121},{2,106},{3,3},{4,20},{5,125},{6,110},{7,7},{8,24},{... | collective-permute-start | bytes 1572872 | tf_op jit(solution)/shard_map/ppermute | solution.py:346
  12.6 3.6 %pick_rows.7 = (bf16[10,16,2048]{2,1,0:T(8,128)(2,1)}, bf16[10,16,2048]{2,1,0:T(8,128)(2,1)}, bf16[10,16,2048]{2,1,0:T(8,128)(2,1)}) custom-call(s32[16]{0:T(128)} %share.7, s32[8]{0:T(128)} %ranks.7, s32[1]{0:T(128)} %bitcast.f_ref, s32[1]{0:T(128)} %bitcast.1.r_ref, bf16[2,512,2048]{2,1,0:T(8,128)(2,1)} %out_hbm.7, bf16[2,1024,2048]{2,1,0:T(8,128)(2,1)} %down_hbm.7), custom_call_target="tpu_custom_call" | custom-call | bytes 5898240 | tf_op jit(solution)/shard_map/pick_rows/pallas_call | solution.py:126
  16.2 0.1 collective-permute-start.9
  16.3 4.6 %collective-permute-start.10 = (bf16[10,16,2048]{2,1,0:T(8,128)(2,1)}, bf16[10,16,2048]{2,1,0:T(8,128)(2,1)S(1)}, u32[]{:S(2)}, u32[]{:S(2)}) collective-permute-start(bf16[10,16,2048]{2,1,0:T(8,128)(2,1)} %get-tuple-element.41), channel_id=1, source_target_pairs={{0,16},{1,121},{2,106},{3,3},{4,20},{5,125},{6,110},{7,7},{8,24},{... | collective-permute-start | bytes 1966088 | tf_op jit(solution)/shard_map/ppermute | solution.py:346
  21.0 3.6 %pick_rows.4 = (bf16[6,16,2048]{2,1,0:T(8,128)(2,1)}, bf16[6,16,2048]{2,1,0:T(8,128)(2,1)}, bf16[6,16,2048]{2,1,0:T(8,128)(2,1)}) custom-call(s32[16]{0:T(128)} %share.7, s32[8]{0:T(128)} %ranks.7, s32[1]{0:T(128)} %bitcast.f_ref, s32[1]{0:T(128)} %bitcast.1.r_ref, bf16[2,512,2048]{2,1,0:T(8,128)(2,1)} %out_hbm.7, bf16[2,1024,2048]{2,1,0:T(8,128)(2,1)} %down_hbm.7), custom_call_target="tpu_custom_call" | custom-call | bytes 3538944 | tf_op jit(solution)/shard_map/pick_rows/pallas_call | solution.py:126
  24.6 2.6 %pick_rows.6.refs_4_ = bf16[8,16,2048]{2,1,0:T(8,128)(2,1)} custom-call(s32[16]{0:T(128)} %share.7, s32[8]{0:T(128)} %ranks.7, s32[1]{0:T(128)} %bitcast.f_ref, s32[1]{0:T(128)} %bitcast.1.r_ref, bf16[2,512,2048]{2,1,0:T(8,128)(2,1)} %out_hbm.7, bf16[2,1024,2048]{2,1,0:T(8,128)(2,1)} %down_hbm.7), custom_call_target="tpu_custom_call" | custom-call | bytes 4718592 | tf_op jit(solution)/shard_map/pick_rows/pallas_call | solution.py:126
  27.2 0.0 collective-permute-done
  27.3 0.0 collective-permute-done.1
  27.3 0.1 pad_maximum_fusion.refs_0_
  27.4 0.0 copy-start.1
  27.4 0.1 collective-permute-start.4
  27.5 0.7 copy-done.5
  28.2 4.6 %collective-permute-start.5 = (bf16[6,16,2048]{2,1,0:T(8,128)(2,1)S(1)}, bf16[6,16,2048]{2,1,0:T(8,128)(2,1)S(1)}, u32[]{:S(2)}, u32[]{:S(2)}) collective-permute-start(bf16[6,16,2048]{2,1,0:T(8,128)(2,1)S(1)} %copy-done.5), channel_id=1, source_target_pairs={{0,16},{1,121},{2,106},{3,3},{4,20},{5,125},{6,110},{7,7},{8,24},{... | collective-permute-start | bytes 1179656 | tf_op jit(solution)/shard_map/ppermute | solution.py:346
  32.8 0.6 collective-permute-start.2
  33.5 0.1 collective-permute-start.12
  33.6 6.8 %collective-permute-start.3 = (bf16[16,16,2048]{2,1,0:T(8,128)(2,1)S(1)}, bf16[16,16,2048]{2,1,0:T(8,128)(2,1)S(1)}, u32[]{:S(2)}, u32[]{:S(2)}) collective-permute-start(bf16[16,16,2048]{2,1,0:T(8,128)(2,1)S(1)} %pad_maximum_fusion.refs_0_), channel_id=1, source_target_pairs={{0,1},{1,0},{2,3},{3,2},{4,5},{5,4},{6,7},{7,6},{8,9},{9,8},{10,11... | collective-permute-start | bytes 3145736 | tf_op jit(solution)/shard_map/ppermute | solution.py:354
  40.4 1.4 %collective-permute-done.2 = bf16[6,16,2048]{2,1,0:T(8,128)(2,1)S(1)} collective-permute-done((bf16[6,16,2048]{2,1,0:T(8,128)(2,1)S(1)}, bf16[6,16,2048]{2,1,0:T(8,128)(2,1)S(1)}, u32[]{:S(2)}, u32[]{:S(2)}) %collective-permute-start.2) | collective-permute-done | bytes 393248 | tf_op jit(solution)/shard_map/ppermute | solution.py:346
  41.7 4.0 %collective-permute-start.6 = (bf16[16,16,2048]{2,1,0:T(8,128)(2,1)S(1)}, bf16[16,16,2048]{2,1,0:T(8,128)(2,1)S(1)}, u32[]{:S(2)}, u32[]{:S(2)}) collective-permute-start(bf16[16,16,2048]{2,1,0:T(8,128)(2,1)S(1)} %collective-permute-done.4.refs_2_), channel_id=1, source_target_pairs={{0,1},{1,0},{2,3},{3,2},{4,5},{5,4},{6,7},{7,6},{8,9},{9,8},{10,11... | collective-permute-start | bytes 3145736 | tf_op jit(solution)/shard_map/ppermute | solution.py:354
  45.7 0.1 collective-permute-start.11
  45.8 2.2 %collective-permute-done.6.refs_3_ = bf16[16,16,2048]{2,1,0:T(8,128)(2,1)S(1)} collective-permute-done((bf16[16,16,2048]{2,1,0:T(8,128)(2,1)S(1)}, bf16[16,16,2048]{2,1,0:T(8,128)(2,1)S(1)}, u32[]{:S(2)}, u32[]{:S(2)}) %collective-permute-start.6) | collective-permute-done | bytes 1048608 | tf_op jit(solution)/shard_map/ppermute | solution.py:354
  48.0 6.2 %rotate_cast.3 = (bf16[256,16384]{1,0:T(8,128)(2,1)}, bf16[256,128]{1,0:T(8,128)(2,1)}) custom-call(s32[1]{0:T(128)} %bitcast.f_ref, s32[1]{0:T(128)} %bitcast.1.r_ref, bf16[16,16,2048]{2,1,0:T(8,128)(2,1)S(1)} %pad_maximum_fusion.refs_0_, bf16[16,16,2048]{2,1,0:T(8,128)(2,1)S(1)} %collective-permute-done.3.refs_1_, ...), custom_call_target="tpu_custom_call" | custom-call | flops 536870912 | bytes 8388608 | tf_op jit(solution)/shard_map/rotate_cast/pallas_call | solution.py:273
  54.2 1.3 %collective-permute-done.12.refs_2_ = bf16[20,16,2048]{2,1,0:T(8,128)(2,1)S(1)} collective-permute-done((bf16[20,16,2048]{2,1,0:T(8,128)(2,1)S(1)}, bf16[20,16,2048]{2,1,0:T(8,128)(2,1)S(1)}, u32[]{:S(2)}, u32[]{:S(2)}) %collective-permute-start.12) | collective-permute-done | bytes 1310752 | tf_op jit(solution)/shard_map/ppermute | solution.py:351
  55.4 4.2 %collective-permute-start.13 = (bf16[20,16,2048]{2,1,0:T(8,128)(2,1)S(1)}, bf16[20,16,2048]{2,1,0:T(8,128)(2,1)S(1)}, u32[]{:S(2)}, u32[]{:S(2)}) collective-permute-start(bf16[20,16,2048]{2,1,0:T(8,128)(2,1)S(1)} %collective-permute-done.12.refs_2_), channel_id=1, source_target_pairs={{0,1},{1,0},{2,3},{3,2},{4,5},{5,4},{6,7},{7,6},{8,9},{9,8},{10,11... | collective-permute-start | bytes 3932168 | tf_op jit(solution)/shard_map/ppermute | solution.py:354
  59.7 0.1 collective-permute-start.8
  59.8 1.0 %collective-permute-start.7 = (bf16[12,16,2048]{2,1,0:T(8,128)(2,1)S(1)}, bf16[12,16,2048]{2,1,0:T(8,128)(2,1)S(1)}, u32[]{:S(2)}, u32[]{:S(2)}) collective-permute-start(bf16[12,16,2048]{2,1,0:T(8,128)(2,1)S(1)} %constant_dynamic-update-slice_fusion.refs_0_), channel_id=1, source_target_pairs={{0,1},{1,0},{2,3},{3,2},{4,5},{5,4},{6,7},{7,6},{8,9},{9,8},{10,11... | collective-permute-start | bytes 2359304 | tf_op jit(solution)/shard_map/ppermute | solution.py:354
  60.7 1.5 %collective-permute-done.13.refs_3_ = bf16[20,16,2048]{2,1,0:T(8,128)(2,1)S(1)} collective-permute-done((bf16[20,16,2048]{2,1,0:T(8,128)(2,1)S(1)}, bf16[20,16,2048]{2,1,0:T(8,128)(2,1)S(1)}, u32[]{:S(2)}, u32[]{:S(2)}) %collective-permute-start.13) | collective-permute-done | bytes 1310752 | tf_op jit(solution)/shard_map/ppermute | solution.py:354
  62.3 7.6 %rotate_cast.4 = (bf16[256,16384]{1,0:T(8,128)(2,1)}, bf16[256,128]{1,0:T(8,128)(2,1)}, bf16[128,16384]{1,0:T(8,128)(2,1)}, bf16[128,128]{1,0:T(8,128)(2,1)}) custom-call(s32[1]{0:T(128)} %bitcast.f_ref, s32[1]{0:T(128)} %bitcast.1.r_ref, ...), custom_call_target="tpu_custom_call", output_to_operand_aliasing={{0}: (8, {}), {1}: (9, {})} | custom-call | flops 671088640 | bytes 10485760 | tf_op jit(solution)/shard_map/rotate_cast/pallas_call | solution.py:273
  69.9 1.9 %collective-permute-done.8.refs_2_ = bf16[12,16,2048]{2,1,0:T(8,128)(2,1)S(1)} collective-permute-done((bf16[12,16,2048]{2,1,0:T(8,128)(2,1)S(1)}, bf16[12,16,2048]{2,1,0:T(8,128)(2,1)S(1)}, u32[]{:S(2)}, u32[]{:S(2)}) %collective-permute-start.8) | collective-permute-done | bytes 786464 | tf_op jit(solution)/shard_map/ppermute | solution.py:351
  71.8 2.3 %collective-permute-done.14.refs_3_ = bf16[12,16,2048]{2,1,0:T(8,128)(2,1)S(1)} collective-permute-done((bf16[12,16,2048]{2,1,0:T(8,128)(2,1)S(1)}, bf16[12,16,2048]{2,1,0:T(8,128)(2,1)S(1)}, u32[]{:S(2)}, u32[]{:S(2)}) %collective-permute-start.14) | collective-permute-done | bytes 786464 | tf_op jit(solution)/shard_map/ppermute | solution.py:354
  74.1 4.9 %rotate_cast.5 = (bf16[128,16384]{1,0:T(8,128)(2,1)}, bf16[128,128]{1,0:T(8,128)(2,1)}) custom-call(s32[1]{0:T(128)} %bitcast.f_ref, s32[1]{0:T(128)} %bitcast.1.r_ref, bf16[12,16,2048]{2,1,0:T(8,128)(2,1)S(1)} %constant_dynamic-update-slice_fusion.refs_0_, ...), custom_call_target="tpu_custom_call", output_to_operand_aliasing={{0}: (8, {}), {1}: (9, {})} | custom-call | flops 402653184 | bytes 6291456 | tf_op jit(solution)/shard_map/rotate_cast/pallas_call | solution.py:273
  (22 shorter events, 0.2 us)
Async XLA Ops:
  3.6 23.7 %collective-permute-start = (bf16[8,16,2048]{2,1,0:T(8,128)(2,1)}, bf16[8,16,2048]{2,1,0:T(8,128)(2,1)S(1)}, u32[]{:S(2)}, u32[]{:S(2)}) collective-permute-start(bf16[8,16,2048]{2,1,0:T(8,128)(2,1)} %get-tuple-element.29), channel_id=1, source_target_pairs={{0,48},{1,81},{2,34},{3,67},{4,52},{5,85},{6,38},{7,71},{8,56},{9,... | collective-permute-start | bytes 1572872 | tf_op jit(solution)/shard_map/ppermute | solution.py:346
  7.1 20.1 %collective-permute-start.1 = (bf16[8,16,2048]{2,1,0:T(8,128)(2,1)}, bf16[8,16,2048]{2,1,0:T(8,128)(2,1)S(1)}, u32[]{:S(2)}, u32[]{:S(2)}) collective-permute-start(bf16[8,16,2048]{2,1,0:T(8,128)(2,1)} %get-tuple-element.30), channel_id=1, source_target_pairs={{0,16},{1,121},{2,106},{3,3},{4,20},{5,125},{6,110},{7,7},{8,24},{... | collective-permute-start | bytes 1572872 | tf_op jit(solution)/shard_map/ppermute | solution.py:346
  16.2 17.2 %collective-permute-start.9 = (bf16[10,16,2048]{2,1,0:T(8,128)(2,1)}, bf16[10,16,2048]{2,1,0:T(8,128)(2,1)S(1)}, u32[]{:S(2)}, u32[]{:S(2)}) collective-permute-start(bf16[10,16,2048]{2,1,0:T(8,128)(2,1)} %get-tuple-element.40), channel_id=1, source_target_pairs={{0,48},{1,81},{2,34},{3,67},{4,52},{5,85},{6,38},{7,71},{8,56},{9,... | collective-permute-start | bytes 1966088 | tf_op jit(solution)/shard_map/ppermute | solution.py:346
  16.3 17.1 %collective-permute-start.10 = (bf16[10,16,2048]{2,1,0:T(8,128)(2,1)}, bf16[10,16,2048]{2,1,0:T(8,128)(2,1)S(1)}, u32[]{:S(2)}, u32[]{:S(2)}) collective-permute-start(bf16[10,16,2048]{2,1,0:T(8,128)(2,1)} %get-tuple-element.41), channel_id=1, source_target_pairs={{0,16},{1,121},{2,106},{3,3},{4,20},{5,125},{6,110},{7,7},{8,24},{... | collective-permute-start | bytes 1966088 | tf_op jit(solution)/shard_map/ppermute | solution.py:346
  27.2 1.0 %copy-start.5 = (bf16[6,16,2048]{2,1,0:T(8,128)(2,1)S(1)}, bf16[6,16,2048]{2,1,0:T(8,128)(2,1)}, u32[]{:S(2)}) copy-start(bf16[6,16,2048]{2,1,0:T(8,128)(2,1)} %get-tuple-element.35) | copy-start | bytes 1179652
  27.2 5.6 %copy-start.4 = (bf16[6,16,2048]{2,1,0:T(8,128)(2,1)S(1)}, bf16[6,16,2048]{2,1,0:T(8,128)(2,1)}, u32[]{:S(2)}) copy-start(bf16[6,16,2048]{2,1,0:T(8,128)(2,1)} %get-tuple-element.34) | copy-start | bytes 1179652
  27.4 20.6 %copy-start = (bf16[8,16,2048]{2,1,0:T(8,128)(2,1)S(1)}, bf16[8,16,2048]{2,1,0:T(8,128)(2,1)}, u32[]{:S(2)}) copy-start(bf16[8,16,2048]{2,1,0:T(8,128)(2,1)} %pick_rows.6.refs_4_) | copy-start | bytes 1572868
  27.4 20.6 %copy-start.1 = (bf16[256,256]{1,0:T(8,128)(2,1)S(1)}, bf16[256,256]{1,0:T(8,128)(2,1)}, u32[]{:S(2)}) copy-start(bf16[256,256]{1,0:T(8,128)(2,1)} %constant.24.clone.refs_5_) | copy-start | bytes 393220
  27.4 14.3 %collective-permute-start.4 = (bf16[16,16,2048]{2,1,0:T(8,128)(2,1)S(1)}, bf16[16,16,2048]{2,1,0:T(8,128)(2,1)S(1)}, u32[]{:S(2)}, u32[]{:S(2)}) collective-permute-start(bf16[16,16,2048]{2,1,0:T(8,128)(2,1)S(1)} %pad_maximum_fusion.refs_0_), channel_id=1, source_target_pairs={{0,2},{1,7},{2,4},{3,1},{4,6},{5,3},{6,0},{7,5},{8,10},{9,15},{10,... | collective-permute-start | bytes 3145736 | tf_op jit(solution)/shard_map/ppermute | solution.py:351
  28.2 12.1 %collective-permute-start.5 = (bf16[6,16,2048]{2,1,0:T(8,128)(2,1)S(1)}, bf16[6,16,2048]{2,1,0:T(8,128)(2,1)S(1)}, u32[]{:S(2)}, u32[]{:S(2)}) collective-permute-start(bf16[6,16,2048]{2,1,0:T(8,128)(2,1)S(1)} %copy-done.5), channel_id=1, source_target_pairs={{0,16},{1,121},{2,106},{3,3},{4,20},{5,125},{6,110},{7,7},{8,24},{... | collective-permute-start | bytes 1179656 | tf_op jit(solution)/shard_map/ppermute | solution.py:346
  32.8 8.9 %collective-permute-start.2 = (bf16[6,16,2048]{2,1,0:T(8,128)(2,1)S(1)}, bf16[6,16,2048]{2,1,0:T(8,128)(2,1)S(1)}, u32[]{:S(2)}, u32[]{:S(2)}) collective-permute-start(bf16[6,16,2048]{2,1,0:T(8,128)(2,1)S(1)} %copy-done.4), channel_id=1, source_target_pairs={{0,48},{1,81},{2,34},{3,67},{4,52},{5,85},{6,38},{7,71},{8,56},{9,... | collective-permute-start | bytes 1179656 | tf_op jit(solution)/shard_map/ppermute | solution.py:346
  33.5 21.9 %collective-permute-start.12 = (bf16[20,16,2048]{2,1,0:T(8,128)(2,1)S(1)}, bf16[20,16,2048]{2,1,0:T(8,128)(2,1)S(1)}, u32[]{:S(2)}, u32[]{:S(2)}) collective-permute-start(bf16[20,16,2048]{2,1,0:T(8,128)(2,1)S(1)} %constant_dynamic-update-slice_fusion.2.refs_0_), channel_id=1, source_target_pairs={{0,2},{1,7},{2,4},{3,1},{4,6},{5,3},{6,0},{7,5},{8,10},{9,15},{10,... | collective-permute-start | bytes 3932168 | tf_op jit(solution)/shard_map/ppermute | solution.py:351
  33.6 12.2 %collective-permute-start.3 = (bf16[16,16,2048]{2,1,0:T(8,128)(2,1)S(1)}, bf16[16,16,2048]{2,1,0:T(8,128)(2,1)S(1)}, u32[]{:S(2)}, u32[]{:S(2)}) collective-permute-start(bf16[16,16,2048]{2,1,0:T(8,128)(2,1)S(1)} %pad_maximum_fusion.refs_0_), channel_id=1, source_target_pairs={{0,1},{1,0},{2,3},{3,2},{4,5},{5,4},{6,7},{7,6},{8,9},{9,8},{10,11... | collective-permute-start | bytes 3145736 | tf_op jit(solution)/shard_map/ppermute | solution.py:354
  41.7 6.3 %collective-permute-start.6 = (bf16[16,16,2048]{2,1,0:T(8,128)(2,1)S(1)}, bf16[16,16,2048]{2,1,0:T(8,128)(2,1)S(1)}, u32[]{:S(2)}, u32[]{:S(2)}) collective-permute-start(bf16[16,16,2048]{2,1,0:T(8,128)(2,1)S(1)} %collective-permute-done.4.refs_2_), channel_id=1, source_target_pairs={{0,1},{1,0},{2,3},{3,2},{4,5},{5,4},{6,7},{7,6},{8,9},{9,8},{10,11... | collective-permute-start | bytes 3145736 | tf_op jit(solution)/shard_map/ppermute | solution.py:354
  45.7 15.0 %collective-permute-start.11 = (bf16[20,16,2048]{2,1,0:T(8,128)(2,1)S(1)}, bf16[20,16,2048]{2,1,0:T(8,128)(2,1)S(1)}, u32[]{:S(2)}, u32[]{:S(2)}) collective-permute-start(bf16[20,16,2048]{2,1,0:T(8,128)(2,1)S(1)} %constant_dynamic-update-slice_fusion.2.refs_0_), channel_id=1, source_target_pairs={{0,1},{1,0},{2,3},{3,2},{4,5},{5,4},{6,7},{7,6},{8,9},{9,8},{10,11... | collective-permute-start | bytes 3932168 | tf_op jit(solution)/shard_map/ppermute | solution.py:354
  54.2 8.1 %copy-start.2 = (bf16[10,16,2048]{2,1,0:T(8,128)(2,1)S(1)}, bf16[10,16,2048]{2,1,0:T(8,128)(2,1)}, u32[]{:S(2)}) copy-start(bf16[10,16,2048]{2,1,0:T(8,128)(2,1)} %get-tuple-element.43.refs_4_) | copy-start | bytes 1966084
  55.4 6.8 %collective-permute-start.13 = (bf16[20,16,2048]{2,1,0:T(8,128)(2,1)S(1)}, bf16[20,16,2048]{2,1,0:T(8,128)(2,1)S(1)}, u32[]{:S(2)}, u32[]{:S(2)}) collective-permute-start(bf16[20,16,2048]{2,1,0:T(8,128)(2,1)S(1)} %collective-permute-done.12.refs_2_), channel_id=1, source_target_pairs={{0,1},{1,0},{2,3},{3,2},{4,5},{5,4},{6,7},{7,6},{8,9},{9,8},{10,11... | collective-permute-start | bytes 3932168 | tf_op jit(solution)/shard_map/ppermute | solution.py:354
  59.7 12.1 %collective-permute-start.8 = (bf16[12,16,2048]{2,1,0:T(8,128)(2,1)S(1)}, bf16[12,16,2048]{2,1,0:T(8,128)(2,1)S(1)}, u32[]{:S(2)}, u32[]{:S(2)}) collective-permute-start(bf16[12,16,2048]{2,1,0:T(8,128)(2,1)S(1)} %constant_dynamic-update-slice_fusion.refs_0_), channel_id=1, source_target_pairs={{0,6},{1,3},{2,0},{3,5},{4,2},{5,7},{6,4},{7,1},{8,14},{9,11},{10,... | collective-permute-start | bytes 2359304 | tf_op jit(solution)/shard_map/ppermute | solution.py:351
  59.8 12.0 %collective-permute-start.7 = (bf16[12,16,2048]{2,1,0:T(8,128)(2,1)S(1)}, bf16[12,16,2048]{2,1,0:T(8,128)(2,1)S(1)}, u32[]{:S(2)}, u32[]{:S(2)}) collective-permute-start(bf16[12,16,2048]{2,1,0:T(8,128)(2,1)S(1)} %constant_dynamic-update-slice_fusion.refs_0_), channel_id=1, source_target_pairs={{0,1},{1,0},{2,3},{3,2},{4,5},{5,4},{6,7},{7,6},{8,9},{9,8},{10,11... | collective-permute-start | bytes 2359304 | tf_op jit(solution)/shard_map/ppermute | solution.py:354
  62.3 11.8 %copy-start.3 = (bf16[6,16,2048]{2,1,0:T(8,128)(2,1)S(1)}, bf16[6,16,2048]{2,1,0:T(8,128)(2,1)}, u32[]{:S(2)}) copy-start(bf16[6,16,2048]{2,1,0:T(8,128)(2,1)} %get-tuple-element.32.refs_4_) | copy-start | bytes 1179652
  71.8 2.3 %collective-permute-start.14 = (bf16[12,16,2048]{2,1,0:T(8,128)(2,1)S(1)}, bf16[12,16,2048]{2,1,0:T(8,128)(2,1)S(1)}, u32[]{:S(2)}, u32[]{:S(2)}) collective-permute-start(bf16[12,16,2048]{2,1,0:T(8,128)(2,1)S(1)} %collective-permute-done.8.refs_2_), channel_id=1, source_target_pairs={{0,1},{1,0},{2,3},{3,2},{4,5},{5,4},{6,7},{7,6},{8,9},{9,8},{10,11... | collective-permute-start | bytes 2359304 | tf_op jit(solution)/shard_map/ppermute | solution.py:354
